TPU v7x, 32 devices: a whole 2x2x4 slice. The times are simulated.
32 devices in a mesh: sub: 16 (over z, x, core), coarse: 2 (over y).
Axes of the slice: x: 2, y: 2, z: 4, core: 2. Of those that a mesh axis runs over, the one named last changes fastest.
Arguments:
- residual_parts: bfloat16 [16, 2, 4, 256, 512], P('sub', 'coarse'), may hold values from -6 to 6
- face_slot: int32 [16, 2, 4], P('sub', 'coarse'), may hold values from 0 to 3, each once within a row
- face_order: int32 [16, 2, 4, 512], P('sub', 'coarse'), may hold values from 0 to 511, each once within a row
- face_scale: float32 [16, 2, 4], P('sub', 'coarse'), may hold values from 0 to 1, as said below
- vertex_unknowns: int32 [16, 2, 256], P('sub', 'coarse'), may hold values from 0 to 2047, all different within a row
- front_inverse: bfloat16 [16, 2, 2048, 2048], P('sub', 'coarse')
- coarse_basis: bfloat16 [16, 2, 2048, 256], P('sub', 'coarse'), may hold values from -0.125 to 0.125
- coarse_inverse: bfloat16 [16, 512, 512], P('sub', None, 'coarse'), as said below
- thermal_handoff: bfloat16 [16, 512, 128], P('sub'), may hold values from -0.25 to 0.25
- chain_transfer: float32 [16, 128, 128], P('sub')
- coupling_in: bfloat16 [16, 128, 512], P('sub', None, 'coarse'), may hold values from -0.5 to 0.5
Outputs:
- correction: bfloat16 [16, 2, 4, 256, 512], P('sub', 'coarse')
Inputs may be any that keep to these rules, and one draw needn't show every extreme that they name: `face_slot`: each row is a permutation of 0 to 3. `face_order`: each row is a permutation of 0 to 511. `vertex_unknowns`: the 256 entries of each subdomain are distinct. `face_scale`: the two weights of a shared face sum to one; a face on the outer boundary has weight one. `coarse_inverse`: each line's matrix is symmetric.
All inputs are finite; a program needn't handle non-finite values.
Results may differ from a plain program's by a relative error of at most 0.0059.
Values may be sent and summed in bfloat16 or wider, within the bound.
A program may use at most 128 MiB of HBM per device.

v0:
```python
import jax
import jax.numpy as jnp
from jax import lax
from jax.sharding import PartitionSpec as P

HIGHEST = lax.Precision.HIGHEST


def with_halo(block, sides, width):
    for axis, dim in sides:
        count = lax.axis_size(axis)
        forward = [(i, i + 1) for i in range(count - 1)]
        backward = [(target, source) for source, target in forward]
        low = lax.ppermute(
            lax.slice_in_dim(block, block.shape[dim] - width, None, axis=dim), axis, forward
        )
        high = lax.ppermute(lax.slice_in_dim(block, 0, width, axis=dim), axis, backward)
        block = jnp.concatenate([low, block, high], axis=dim)
    return block


def carried_in(array, axis, combine, identity):
    peers, mine = (lax.axis_size(axis), lax.axis_index(axis))
    everything = jax.tree.map(lambda part: lax.all_gather(part, axis), array)
    start = jax.tree.map(
        lambda part, zero: jnp.broadcast_to(jnp.asarray(zero, part.dtype), part.shape),
        array,
        identity,
    )

    def step(k, before):
        reached = k < mine
        new = combine(before, jax.tree.map(lambda part: part[k], everything))
        return jax.tree.map(lambda a, b: jnp.where(reached, a, b), new, before)

    return lax.fori_loop(0, peers, step, start)


def build_tables(face_slot, face_order, table_type):
    face_count, block_size = face_order.shape
    slot_table = (
        face_slot[:, None] == lax.broadcasted_iota(jnp.int32, (face_count, face_count), 1)
    ).astype(table_type)
    order_table = (
        face_order[:, :, None]
        == lax.broadcasted_iota(jnp.int32, (face_count, block_size, block_size), 2)
    ).astype(table_type)
    return (slot_table, order_table)


def to_canonical(values, tables):
    slot_table, order_table = tables
    ordered = jnp.einsum(
        "snk,sjk->snj", values, order_table, preferred_element_type=jnp.float32, precision=HIGHEST
    ).astype(values.dtype)
    return jnp.einsum(
        "ds,snj->dnj", slot_table, ordered, preferred_element_type=jnp.float32, precision=HIGHEST
    ).astype(values.dtype)


def from_canonical(values, tables):
    slot_table, order_table = tables
    by_face = jnp.einsum(
        "ds,dnj->snj", slot_table, values, preferred_element_type=jnp.float32, precision=HIGHEST
    ).astype(values.dtype)
    return jnp.einsum(
        "snj,sjk->snk", by_face, order_table, preferred_element_type=jnp.float32, precision=HIGHEST
    ).astype(values.dtype)


def trade_faces(face_values):
    along_sub = with_halo(face_values[0:2], (("sub", 0),), 1)
    along_coarse = with_halo(face_values[2:4], (("coarse", 0),), 1)
    return jnp.stack([along_sub[0], along_sub[3], along_coarse[0], along_coarse[3]], 0)


def per_device(
    residual_parts,
    face_slot,
    face_order,
    face_scale,
    vertex_unknowns,
    front_inverse,
    coarse_basis,
    coarse_inverse,
    thermal_handoff,
    chain_transfer,
    coupling_in,
):
    own_parts = residual_parts[0, 0]
    own_slot = face_slot[0, 0]
    own_order = face_order[0, 0]
    own_scale = face_scale[0, 0][:, None, None]
    face_count, sample_count, block_size = own_parts.shape
    reduced_precision_tables = build_tables(own_slot, own_order, jnp.bfloat16)
    canon = to_canonical(own_parts, reduced_precision_tables)
    beside = trade_faces(canon)
    averaged = (own_scale * (canon.astype(jnp.float32) + beside.astype(jnp.float32))).astype(
        jnp.bfloat16
    )
    local_residual = from_canonical(averaged, reduced_precision_tables)
    own_primal = vertex_unknowns[0, 0]
    positions = lax.broadcasted_iota(jnp.int32, (own_primal.shape[0], face_count * block_size), 1)
    hits = jnp.sum((own_primal[:, None] == positions).astype(jnp.int32), axis=0)
    dual_mask = (1 - hits).astype(jnp.bfloat16).reshape(face_count, 1, block_size)
    inverse_blocks = front_inverse[0, 0].reshape(face_count, block_size, face_count, block_size)
    dual_part = (
        jnp.einsum(
            "gnj,gjfk->fnk",
            local_residual * dual_mask,
            inverse_blocks,
            preferred_element_type=jnp.float32,
        )
        * dual_mask
    )
    basis_blocks = coarse_basis[0, 0].reshape(face_count, block_size, -1)
    coarse_residual = jnp.einsum(
        "gnj,gjc->nc", local_residual, basis_blocks, preferred_element_type=jnp.float32
    ).astype(jnp.bfloat16)
    primal_count = coarse_residual.shape[1]
    line_block = coarse_inverse[0]
    line_outflow = thermal_handoff[0]
    channel_count = line_outflow.shape[1]
    line_base = lax.dot_general(
        line_block,
        lax.all_gather(coarse_residual, "coarse", axis=1, tiled=True),
        (((0,), (1,)), ((), ())),
        preferred_element_type=jnp.float32,
    )
    own_rows = lax.dynamic_slice_in_dim(
        line_outflow, lax.axis_index("coarse") * primal_count, primal_count, 0
    )
    inflow = lax.psum(
        jnp.dot(coarse_residual, own_rows, preferred_element_type=jnp.float32), "coarse"
    )
    transfer = chain_transfer[0]

    def compose(earlier, later):
        joined_map = jnp.dot(earlier[0], later[0], precision=HIGHEST)
        joined_state = jnp.dot(earlier[1], later[0], precision=HIGHEST) + later[1]
        return (joined_map, joined_state)

    identity = (jnp.eye(channel_count, dtype=jnp.float32), jnp.zeros_like(inflow))
    upstream_map, carried = carried_in((transfer, inflow), "sub", compose, identity)
    carried_term = lax.dot_general(
        coupling_in[0].astype(jnp.float32), carried, (((0,), (1,)), ((), ())), precision=HIGHEST
    )
    global_coarse_answer = (line_base + carried_term).astype(jnp.bfloat16)
    subregion_iterate = dual_part + jnp.einsum(
        "cn,gjc->gnj", global_coarse_answer, basis_blocks, preferred_element_type=jnp.float32
    )
    exact_tables = build_tables(own_slot, own_order, jnp.float32)
    weighted = (own_scale * to_canonical(subregion_iterate, exact_tables)).astype(jnp.bfloat16)
    beside_again = trade_faces(weighted)
    summed = (weighted.astype(jnp.float32) + beside_again.astype(jnp.float32)).astype(jnp.bfloat16)
    return from_canonical(summed, reduced_precision_tables)[None, None]


def solution(mesh):
    placed = (
        P("sub", "coarse", None, None, None),
        P("sub", "coarse", None),
        P("sub", "coarse", None, None),
        P("sub", "coarse", None),
        P("sub", "coarse", None),
        P("sub", "coarse", None, None),
        P("sub", "coarse", None, None),
        P("sub", None, "coarse"),
        P("sub", None, None),
        P("sub", None, None),
        P("sub", None, "coarse"),
    )
    return jax.shard_map(
        per_device,
        mesh=mesh,
        in_specs=placed,
        out_specs=P("sub", "coarse", None, None, None),
        check_vma=False,
    )
```

profile of v0, /device:TPU:0, one launch (start us, length us, event | category | flops | bytes accessed | tf_op | source)
XLA Modules:
  0.0 213.7 jit_solution(4002481424145081081)
XLA Ops:
  7.4 2.4 %fusion.30 = bf16[4,256,512]{1,2,0:T(8,128)(2,1)S(1)} fusion(s32[4,512]{1,0:T(4,128)} %bitcast.80, bf16[1,1,4,256,512]{4,3,2,1,0:T(8,128)(2,1)} %param.13), kind=kOutput, calls=%fused_computation.39 | convolution fusion | flops 538443776 | bytes 2105344 | tf_op jit(solution)/shard_map/snk,sjk->snj/dot_general | solution.py:53
  9.8 1.0 copy.15
  10.8 1.1 convolution_convert_fusion.2
  11.9 2.3 %fusion.70 = (bf16[1,256,512]{2,0,1:T(2,128)(2,1)}, bf16[1,256,512]{2,0,1:T(2,128)(2,1)S(1)}, bf16[1,256,512]{2,0,1:T(2,128)(2,1)S(1)}, bf16[1,256,512]{2,0,1:T(2,128)(2,1)}) fusion(bf16[4,256,512]{2,0,1:T(4,128)(2,1)S(1)} %convolution_convert_fusion.2), kind=kLoop, calls=%fused_computation.80 | loop fusion | bytes 2097152 | tf_op jit(solution)/shard_map/slice | solution.py:15
  14.3 3.2 %collective-permute-start = (bf16[1,256,512]{2,0,1:T(2,128)(2,1)}, bf16[1,256,512]{2,0,1:T(2,128)(2,1)}, u32[]{:S(2)}, u32[]{:S(2)}) collective-permute-start(bf16[1,256,512]{2,0,1:T(2,128)(2,1)} %get-tuple-element.147), channel_id=1, source_target_pairs={{0,2},{2,4},{4,6},{6,8},{8,10},{10,12},{12,14},{14,16},{16,18},{18... | collective-permute-start | bytes 786440 | tf_op jit(solution)/shard_map/ppermute | solution.py:14
  17.4 1.3 collective-permute-start.1
  18.7 5.1 %collective-permute-start.2 = (bf16[1,256,512]{2,0,1:T(2,128)(2,1)S(1)}, bf16[1,256,512]{2,0,1:T(2,128)(2,1)}, u32[]{:S(2)}, u32[]{:S(2)}) collective-permute-start(bf16[1,256,512]{2,0,1:T(2,128)(2,1)S(1)} %get-tuple-element.149), channel_id=1, source_target_pairs={{0,1},{2,3},{4,5},{6,7},{8,9},{10,11},{12,13},{14,15},{16,17},{18,... | collective-permute-start | bytes 786440 | tf_op jit(solution)/shard_map/ppermute | solution.py:14
  23.8 1.3 collective-permute-start.3
  25.1 9.6 %collective-permute-done.2 = bf16[1,256,512]{2,0,1:T(2,128)(2,1)} collective-permute-done((bf16[1,256,512]{2,0,1:T(2,128)(2,1)S(1)}, bf16[1,256,512]{2,0,1:T(2,128)(2,1)}, u32[]{:S(2)}, u32[]{:S(2)}) %collective-permute-start.2) | collective-permute-done | bytes 262176 | tf_op jit(solution)/shard_map/ppermute | solution.py:14
  34.7 5.6 %collective-permute-done.3 = bf16[1,256,512]{2,0,1:T(2,128)(2,1)} collective-permute-done((bf16[1,256,512]{2,0,1:T(2,128)(2,1)S(1)}, bf16[1,256,512]{2,0,1:T(2,128)(2,1)}, u32[]{:S(2)}, u32[]{:S(2)}) %collective-permute-start.3) | collective-permute-done | bytes 262176 | tf_op jit(solution)/shard_map/ppermute | solution.py:17
  40.3 4.5 %convolution_convert_fusion.1 = bf16[4,256,512]{2,0,1:T(4,128)(2,1)S(1)} fusion(bf16[4,256,512]{2,0,1:T(4,128)(2,1)S(1)} %convolution_convert_fusion.2, bf16[1,256,512]{2,0,1:T(2,128)(2,1)} %collective-permute-done.3, bf16[1,256,512]{2,0,1:T(2,128)(2,1)} %collective-permute-done.2, bf16[1,256,512]{2,0,1:T(2,128)(2,1)} %collective-permute-done.1, ...), kind=kOutput, calls=%fused_computation.36 | convolution fusion | flops 11010064 | bytes 3145760 | tf_op jit(solution)/shard_map/ds,dnj->snj/dot_general | solution.py:63
  44.8 1.4 fusion.27
  46.2 0.9 copy-done.1
  49.1 21.6 %all-reduce.2.cloned.1.call-done = f32[1,256,128]{2,1,0:T(8,128)} async-done(((f32[1,256,128]{2,1,0:T(8,128)}), f32[1,256,128]{2,1,0:T(8,128)}) %all-reduce.2.cloned.1.call-update) | async-done | bytes 131088 | tf_op jit(solution)/shard_map/psum | solution.py:133
  71.1 14.7 %reshape_squeeze.6 = bf16[4,512,4,512]{3,2,1,0:T(4,128)(2,1)} reshape(bf16[1,1,2048,2048]{3,2,1,0:T(8,128)(2,1)} %param.18) | data formatting | bytes 16777216 | tf_op jit(solution)/shard_map/reshape;squeeze | solution.py:106
  85.8 5.8 %all_gather.12 = bf16[256,512]{1,0:T(8,128)(2,1)S(1)} all-gather(bf16[256,256]{1,0:T(8,128)(2,1)S(1)} %fusion.32), channel_id=1, replica_groups=mesh['sub'=16,'coarse'=2] {'coarse'}, dimensions={1}, use_global_device_ids=true | all-gather | bytes 393216 | tf_op jit(solution)/shard_map/all_gather | solution.py:126
  91.7 0.9 fusion.56
  92.6 6.5 %fusion.9 = f32[256,4,512,1]{2,0,3,1:T(8,128)S(1)} fusion(bf16[4,512,4,512]{3,2,1,0:T(4,128)(2,1)} %reshape_squeeze.6, bf16[4,256,512]{2,1,0:T(8,128)(2,1)} %copy-done.1, bf16[4,512]{1,0:T(4,128)(2,1)S(1)} %convert_element_type.89), kind=kOutput, calls=%fused_computation.11 | convolution fusion | flops 2149580800 | bytes 11538432 | tf_op jit(solution)/shard_map/gnj,gjfk->fnk/dot_general | solution.py:108
  99.2 33.4 %all-gather.5.cloned.1.call-done = f32[16,256,128]{2,1,0:T(8,128)} async-done(((f32[1,256,128]{2,1,0:T(8,128)}), f32[16,256,128]{2,1,0:T(8,128)}) %all-gather.5.cloned.1.call-update) | async-done | bytes 2097168 | tf_op jit(solution)/shard_map/all_gather | solution.py:24
  132.5 35.6 %while.14 = (s32[]{:T(128)}, f32[256,128]{0,1:T(8,128)S(1)}, s32[]{:T(128)}, f32[16,128,128]{2,1,0:T(8,128)}, f32[16,256,128]{2,1,0:T(8,128)}, /*index=5*/s32[]{:T(128)}, s32[]{:T(128)}) while((s32[]{:T(128)}, f32[256,128]{0,1:T(8,128)S(1)}, s32[]{:T(128)}, f32[16,128,128]{2,1,0:T(8,128)}, f32[16,256,128]{2,1,0:T(8,128)}, ...), condition=%wide.region_3.4_spmd.clone, body=%wide.region_2.3_spmd.clone.sunk | while | flops 50462724 | bytes 1378403 | solution.py:36
  133.6 1.2 fusion.85
  135.8 1.2 fusion.85
  138.0 1.2 fusion.85
  140.3 1.2 fusion.85
  142.5 1.2 fusion.85
  144.7 1.2 fusion.85
  147.0 1.2 fusion.85
  149.2 1.2 fusion.85
  151.4 1.2 fusion.85
  153.6 1.2 fusion.85
  155.9 1.2 fusion.85
  158.1 1.2 fusion.85
  160.3 1.2 fusion.85
  162.5 1.2 fusion.85
  164.8 1.2 fusion.85
  167.0 1.2 fusion.85
  168.2 1.3 fusion.33
  170.0 2.8 %fusion.12 = f32[4,256,512]{2,1,0:T(8,128)S(1)} fusion(f32[256,4,512]{2,0,1:T(8,128)S(1)} %fusion.71, f32[256,4,512,1]{2,0,3,1:T(8,128)S(1)} %fusion.9, s32[4,512]{1,0:T(4,128)S(1)} %bitcast.82, f32[4,512]{1,0:T(4,128)S(1)} %convert_element_type.90), kind=kOutput, calls=%fused_computation.15 | convolution fusion | flops 3223322624 | bytes 6307840 | tf_op jit(solution)/shard_map/snk,sjk->snj/dot_general | solution.py:53
  172.8 3.3 %multiply_convert_fusion = bf16[4,256,512]{2,0,1:T(4,128)(2,1)S(1)} fusion(f32[4,256,512]{2,1,0:T(8,128)S(1)} %fusion.12, f32[4]{0:T(128)S(1)} %bitcast.90, s32[4]{0:T(128)S(1)} %bitcast.86), kind=kOutput, calls=%fused_computation.24 | convolution fusion | flops 26214416 | bytes 3145760 | tf_op jit(solution)/shard_map/ds,snj->dnj/dot_general | solution.py:56
  176.1 1.6 fusion.69
  177.7 2.2 %collective-permute-start.4 = (bf16[1,256,512]{2,0,1:T(2,128)(2,1)S(1)}, bf16[1,256,512]{2,0,1:T(2,128)(2,1)S(1)}, u32[]{:S(2)}, u32[]{:S(2)}) collective-permute-start(bf16[1,256,512]{2,0,1:T(2,128)(2,1)S(1)} %get-tuple-element.143), channel_id=1, source_target_pairs={{0,2},{2,4},{4,6},{6,8},{8,10},{10,12},{12,14},{14,16},{16,18},{18... | collective-permute-start | bytes 786440 | tf_op jit(solution)/shard_map/ppermute | solution.py:14
  179.9 1.3 collective-permute-start.5
  181.2 3.4 %collective-permute-start.6 = (bf16[1,256,512]{2,0,1:T(2,128)(2,1)S(1)}, bf16[1,256,512]{2,0,1:T(2,128)(2,1)S(1)}, u32[]{:S(2)}, u32[]{:S(2)}) collective-permute-start(bf16[1,256,512]{2,0,1:T(2,128)(2,1)S(1)} %get-tuple-element.145), channel_id=1, source_target_pairs={{0,1},{2,3},{4,5},{6,7},{8,9},{10,11},{12,13},{14,15},{16,17},{18,... | collective-permute-start | bytes 786440 | tf_op jit(solution)/shard_map/ppermute | solution.py:14
  184.6 1.3 collective-permute-start.7
  185.9 10.8 %collective-permute-done.6 = bf16[1,256,512]{2,0,1:T(2,128)(2,1)S(1)} collective-permute-done((bf16[1,256,512]{2,0,1:T(2,128)(2,1)S(1)}, bf16[1,256,512]{2,0,1:T(2,128)(2,1)S(1)}, u32[]{:S(2)}, u32[]{:S(2)}) %collective-permute-start.6) | collective-permute-done | bytes 262176 | tf_op jit(solution)/shard_map/ppermute | solution.py:14
  196.7 4.5 %collective-permute-done.7 = bf16[1,256,512]{2,0,1:T(2,128)(2,1)S(1)} collective-permute-done((bf16[1,256,512]{2,0,1:T(2,128)(2,1)S(1)}, bf16[1,256,512]{2,0,1:T(2,128)(2,1)S(1)}, u32[]{:S(2)}, u32[]{:S(2)}) %collective-permute-start.7) | collective-permute-done | bytes 262176 | tf_op jit(solution)/shard_map/ppermute | solution.py:17
  201.2 2.9 %convolution_convert_fusion = bf16[4,256,512]{2,0,1:T(4,128)(2,1)S(1)} fusion(bf16[4,256,512]{2,0,1:T(4,128)(2,1)S(1)} %multiply_convert_fusion, bf16[1,256,512]{2,0,1:T(2,128)(2,1)S(1)} %collective-permute-done.7, bf16[1,256,512]{2,0,1:T(2,128)(2,1)S(1)} %collective-permute-done.6, bf16[1,256,512]{2,0,1:T(2,128)(2,1)S(1)} %collective-permute-done.5, ...), kind=kOutput, calls=%fused_computation.35 | convolution fusion | flops 10485776 | bytes 3145744 | tf_op jit(solution)/shard_map/ds,dnj->snj/dot_general | solution.py:63
  204.1 2.2 %fusion.29 = bf16[1,1,4,256,512]{4,3,2,1,0:T(8,128)(2,1)} fusion(s32[4,512]{1,0:T(4,128)S(1)} %bitcast.83, bf16[4,256,512]{2,0,1:T(4,128)(2,1)S(1)} %convolution_convert_fusion), kind=kOutput, calls=%fused_computation.38 | convolution fusion | flops 538443776 | bytes 2105344 | tf_op jit(solution)/shard_map/snj,sjk->snk/dot_general | solution.py:66
  (86 shorter events, 19.2 us)
Async XLA Ops:
  7.4 38.8 %copy-start = (bf16[1,1,2048,256]{3,2,1,0:T(8,128)(2,1)S(1)}, bf16[1,1,2048,256]{3,2,1,0:T(8,128)(2,1)}, u32[]{:S(2)}) copy-start(bf16[1,1,2048,256]{3,2,1,0:T(8,128)(2,1)} %param.19) | copy-start | bytes 3145732
  7.4 63.3 %all-reduce.2.cloned.1.call-start = ((), (), s32[]{:S(2)}) async-start(), calls=%async_computation.1 | async-start | bytes 262144 | tf_op jit(solution)/shard_map/psum | solution.py:133
  7.4 3.5 %copy-start.5 = (s32[1,1,4]{2,1,0:T(1,128)S(1)}, s32[1,1,4]{2,1,0:T(1,128)}, u32[]{:S(2)}) copy-start(s32[1,1,4]{2,1,0:T(1,128)} %param.14) | copy-start | bytes 52
  11.9 28.4 %copy-start.8 = (f32[1,1,4]{2,1,0:T(1,128)S(1)}, f32[1,1,4]{2,1,0:T(1,128)}, u32[]{:S(2)}) copy-start(f32[1,1,4]{2,1,0:T(1,128)} %param.16) | copy-start | bytes 52
  14.3 10.8 %collective-permute-start = (bf16[1,256,512]{2,0,1:T(2,128)(2,1)}, bf16[1,256,512]{2,0,1:T(2,128)(2,1)}, u32[]{:S(2)}, u32[]{:S(2)}) collective-permute-start(bf16[1,256,512]{2,0,1:T(2,128)(2,1)} %get-tuple-element.147), channel_id=1, source_target_pairs={{0,2},{2,4},{4,6},{6,8},{8,10},{10,12},{12,14},{14,16},{16,18},{18... | collective-permute-start | bytes 786440 | tf_op jit(solution)/shard_map/ppermute | solution.py:14
  17.4 7.6 %collective-permute-start.1 = (bf16[1,256,512]{2,0,1:T(2,128)(2,1)}, bf16[1,256,512]{2,0,1:T(2,128)(2,1)}, u32[]{:S(2)}, u32[]{:S(2)}) collective-permute-start(bf16[1,256,512]{2,0,1:T(2,128)(2,1)} %get-tuple-element.150), channel_id=1, source_target_pairs={{2,0},{4,2},{6,4},{8,6},{10,8},{12,10},{14,12},{16,14},{18,16},{20... | collective-permute-start | bytes 786440 | tf_op jit(solution)/shard_map/ppermute | solution.py:17
  18.7 16.0 %collective-permute-start.2 = (bf16[1,256,512]{2,0,1:T(2,128)(2,1)S(1)}, bf16[1,256,512]{2,0,1:T(2,128)(2,1)}, u32[]{:S(2)}, u32[]{:S(2)}) collective-permute-start(bf16[1,256,512]{2,0,1:T(2,128)(2,1)S(1)} %get-tuple-element.149), channel_id=1, source_target_pairs={{0,1},{2,3},{4,5},{6,7},{8,9},{10,11},{12,13},{14,15},{16,17},{18,... | collective-permute-start | bytes 786440 | tf_op jit(solution)/shard_map/ppermute | solution.py:14
  23.8 16.5 %collective-permute-start.3 = (bf16[1,256,512]{2,0,1:T(2,128)(2,1)S(1)}, bf16[1,256,512]{2,0,1:T(2,128)(2,1)}, u32[]{:S(2)}, u32[]{:S(2)}) collective-permute-start(bf16[1,256,512]{2,0,1:T(2,128)(2,1)S(1)} %get-tuple-element.148), channel_id=1, source_target_pairs={{1,0},{3,2},{5,4},{7,6},{9,8},{11,10},{13,12},{15,14},{17,16},{19,... | collective-permute-start | bytes 786440 | tf_op jit(solution)/shard_map/ppermute | solution.py:17
  40.3 4.5 %copy-start.4 = (s32[1,1,4,512]{3,2,1,0:T(4,128)S(1)}, s32[1,1,4,512]{3,2,1,0:T(4,128)}, u32[]{:S(2)}) copy-start(s32[1,1,4,512]{3,2,1,0:T(4,128)} %param.15) | copy-start | bytes 24580
  46.2 1.0 copy-start.1
  46.2 1.4 copy-start.3
  46.2 24.6 %copy-start.7 = (s32[1,1,256]{2,1,0:T(1,128)S(1)}, s32[1,1,256]{2,1,0:T(1,128)}, u32[]{:S(2)}) copy-start(s32[1,1,256]{2,1,0:T(1,128)} %param.17) | copy-start | bytes 3076
  48.4 50.7 %all-gather.3.cloned.1.call-start = ((), (), s32[]{:S(2)}) async-start(), calls=%async_computation | async-start | bytes 1114112 | tf_op jit(solution)/shard_map/all_gather | solution.py:24
  49.0 83.5 %all-gather.5.cloned.1.call-start = ((), (), s32[]{:S(2)}) async-start(), calls=%async_computation.2 | async-start | bytes 2228224 | tf_op jit(solution)/shard_map/all_gather | solution.py:24
  71.1 20.5 %copy-start.2 = (bf16[1,512,256]{2,1,0:T(8,128)(2,1)S(1)}, bf16[1,512,256]{2,1,0:T(8,128)(2,1)}, u32[]{:S(2)}) copy-start(bf16[1,512,256]{2,1,0:T(8,128)(2,1)} %param.20) | copy-start | bytes 786436
  170.0 2.8 %copy-start.6 = (s32[1,1,4]{2,1,0:T(1,128)S(1)}, s32[1,1,4]{2,1,0:T(1,128)}, u32[]{:S(2)}) copy-start(s32[1,1,4]{2,1,0:T(1,128)} %param.14) | copy-start | bytes 52
  170.0 2.8 %copy-start.9 = (f32[1,1,4]{2,1,0:T(1,128)S(1)}, f32[1,1,4]{2,1,0:T(1,128)}, u32[]{:S(2)}) copy-start(f32[1,1,4]{2,1,0:T(1,128)} %param.16) | copy-start | bytes 52
  177.7 8.2 %collective-permute-start.4 = (bf16[1,256,512]{2,0,1:T(2,128)(2,1)S(1)}, bf16[1,256,512]{2,0,1:T(2,128)(2,1)S(1)}, u32[]{:S(2)}, u32[]{:S(2)}) collective-permute-start(bf16[1,256,512]{2,0,1:T(2,128)(2,1)S(1)} %get-tuple-element.143), channel_id=1, source_target_pairs={{0,2},{2,4},{4,6},{6,8},{8,10},{10,12},{12,14},{14,16},{16,18},{18... | collective-permute-start | bytes 786440 | tf_op jit(solution)/shard_map/ppermute | solution.py:14
  179.9 6.0 %collective-permute-start.5 = (bf16[1,256,512]{2,0,1:T(2,128)(2,1)S(1)}, bf16[1,256,512]{2,0,1:T(2,128)(2,1)S(1)}, u32[]{:S(2)}, u32[]{:S(2)}) collective-permute-start(bf16[1,256,512]{2,0,1:T(2,128)(2,1)S(1)} %get-tuple-element.146), channel_id=1, source_target_pairs={{2,0},{4,2},{6,4},{8,6},{10,8},{12,10},{14,12},{16,14},{18,16},{20... | collective-permute-start | bytes 786440 | tf_op jit(solution)/shard_map/ppermute | solution.py:17
  181.2 15.5 %collective-permute-start.6 = (bf16[1,256,512]{2,0,1:T(2,128)(2,1)S(1)}, bf16[1,256,512]{2,0,1:T(2,128)(2,1)S(1)}, u32[]{:S(2)}, u32[]{:S(2)}) collective-permute-start(bf16[1,256,512]{2,0,1:T(2,128)(2,1)S(1)} %get-tuple-element.145), channel_id=1, source_target_pairs={{0,1},{2,3},{4,5},{6,7},{8,9},{10,11},{12,13},{14,15},{16,17},{18,... | collective-permute-start | bytes 786440 | tf_op jit(solution)/shard_map/ppermute | solution.py:14
  184.6 16.6 %collective-permute-start.7 = (bf16[1,256,512]{2,0,1:T(2,128)(2,1)S(1)}, bf16[1,256,512]{2,0,1:T(2,128)(2,1)S(1)}, u32[]{:S(2)}, u32[]{:S(2)}) collective-permute-start(bf16[1,256,512]{2,0,1:T(2,128)(2,1)S(1)} %get-tuple-element.144), channel_id=1, source_target_pairs={{1,0},{3,2},{5,4},{7,6},{9,8},{11,10},{13,12},{15,14},{17,16},{19,... | collective-permute-start | bytes 786440 | tf_op jit(solution)/shard_map/ppermute | solution.py:17
Sparse Core Ops, SparseCore 0:
  48.6 22.0 all-reduce.1
Sparse Core Ops, SparseCore 1:
  51.1 38.8 all-gather.2
  91.9 40.6 all-gather.4
where the time goes:
time: 215 us; the launch traced here: 214 us
  waiting for transfers between devices  86 us (40%)
  matrix products  49.5 us (23%)
  local copies, waits for them, and re-layouts  37 us (17%)
  starting transfers between devices  19 us (9%)
  between operations  15.2 us (7%)
  blocking collectives  5.81 us (3%)
    all_gather x2, waiting for transfers between devices, carried_in(): everything = jax.tree.map(lambda part: lax.all_gather(part, axis), array)  33.4 us
    psum x1, waiting for transfers between devices, per_device(): lax.psum(jnp.dot(coarse_residual, own_rows, preferred_element_type=jnp.fl...  21.6 us
    ppermute x4, waiting for transfers between devices, with_halo(): lax.ppermute(lax.slice_in_dim(block, block.shape[dim] - width, None, axis...  20.4 us
    dot_general x16, matrix products, compose(): joined_state = jnp.dot(earlier[1], later[0], precision=HIGHEST) + later[1]  18.5 us
    dynamic_slice x32, local copies, waits for them, and re-layouts, step(): new = combine(before, jax.tree.map(lambda part: part[k], everything))  16.2 us
    another operation x1, local copies, waits for them, and re-layouts, per_device(): front_inverse[0, 0].reshape(face_count, block_size, face_count, block_size)  14.7 us
    ppermute x4, starting transfers between devices, with_halo(): lax.ppermute(lax.slice_in_dim(block, block.shape[dim] - width, None, axis...  13.8 us
    ppermute x4, waiting for transfers between devices, with_halo(): lax.ppermute(lax.slice_in_dim(block, 0, width, axis=dim), axis, backward)  10.1 us
  transfers between devices with their start and end apart: 11, of which 6 were waited for; matrix products, arithmetic and copies ran while one was open for 11% of the time, Pallas kernels for 0%

commit v1 on v0

v1 whole, which is shorter than its diff:
```python
import jax
import jax.numpy as jnp
from jax import lax
from jax.sharding import PartitionSpec as P

HIGHEST = lax.Precision.HIGHEST


def one_hot_rows(order, count):
    return (
        order[:, None, :] == lax.broadcasted_iota(jnp.int32, (order.shape[0], count, order.shape[1]), 1)
    ).astype(jnp.bfloat16)


def shifted(array, axis, step):
    count = lax.axis_size(axis)
    pairs = [(i, i + step) for i in range(count) if 0 <= i + step < count]
    return lax.ppermute(array, axis, pairs)


def trade(by_direction):
    return [
        shifted(by_direction[1], "sub", 1),
        shifted(by_direction[0], "sub", -1),
        shifted(by_direction[3], "coarse", 1),
        shifted(by_direction[2], "coarse", -1),
    ]


def per_device(
    residual_parts,
    face_slot,
    face_order,
    face_scale,
    vertex_unknowns,
    front_inverse,
    coarse_basis,
    coarse_inverse,
    thermal_handoff,
    chain_transfer,
    coupling_in,
):
    f32, bf16 = jnp.float32, jnp.bfloat16
    parts = residual_parts[0, 0]
    slot = face_slot[0, 0]
    scale = face_scale[0, 0]
    face_count, sample_count, block_size = parts.shape
    by_slot = jnp.argsort(slot)
    order = face_order[0, 0]
    own_canon_order = jnp.stack([order[slot[d]] for d in range(4)])
    own_faces = [parts[slot[d]] for d in range(4)]
    transfer = chain_transfer[0]
    peers, mine = lax.axis_size("sub"), lax.axis_index("sub")
    transfers = lax.all_gather(transfer, "sub")
    their_orders = jnp.stack(trade([own_canon_order[d] for d in range(4)]))
    theirs = trade(own_faces)
    own_table = one_hot_rows(own_canon_order, block_size)
    high, low = (their_orders >> 4).astype(bf16), (their_orders & 15).astype(bf16)
    comp = jnp.einsum("dxj,dkj->dxk", jnp.stack([high, low], 1), own_table, preferred_element_type=f32)
    comp = (comp[:, 0] * 16 + comp[:, 1]).astype(jnp.int32)
    tables = one_hot_rows(comp, block_size)
    rows = [scale[d] * (
        own_faces[d].astype(f32)
        + jnp.dot(theirs[d], tables[d], preferred_element_type=f32)
    ) for d in range(4)]
    averaged = [row.astype(bf16) for row in rows]
    local_residual = jnp.stack(averaged)[by_slot]
    own_primal = vertex_unknowns[0, 0]
    positions = lax.broadcasted_iota(jnp.int32, (own_primal.shape[0], face_count * block_size), 1)
    hits = jnp.sum((own_primal[:, None] == positions).astype(jnp.int32), axis=0)
    dual_mask = (1 - hits).astype(bf16)
    flat = local_residual.transpose(1, 0, 2).reshape(sample_count, face_count * block_size)
    basis = coarse_basis[0, 0]
    coarse_residual = jnp.dot(flat, basis, preferred_element_type=f32).astype(bf16)
    primal_count = coarse_residual.shape[1]
    own_rows = lax.dynamic_slice_in_dim(
        thermal_handoff[0], lax.axis_index("coarse") * primal_count, primal_count, 0
    )
    line_residual = lax.all_gather(coarse_residual, "coarse", axis=1, tiled=True)
    inflow = jnp.dot(line_residual, thermal_handoff[0], preferred_element_type=f32)
    inflows = lax.all_gather(inflow.astype(bf16), "sub")
    dual_part = jnp.dot(flat * dual_mask, front_inverse[0, 0], preferred_element_type=f32) * dual_mask.astype(f32)
    channels = transfer.shape[0]
    eye = jnp.eye(channels, dtype=f32)
    index = lax.broadcasted_iota(jnp.int32, (peers, 1, 1), 0)
    chain = jnp.where(index < mine, transfers, eye)
    step = 1
    while step < peers:
        later = jnp.concatenate([chain[step:], jnp.broadcast_to(eye, (step, channels, channels))], 0)
        chain = jnp.einsum("pab,pbc->pac", chain, later, precision=HIGHEST)
        step *= 2
    weights = jnp.concatenate([chain[1:], eye[None]], 0)
    weights = jnp.where(index < mine, weights, 0.0).astype(bf16)
    carried = jnp.einsum("pna,pac->nc", inflows, weights, preferred_element_type=f32)
    line_base = jnp.dot(line_residual, coarse_inverse[0], preferred_element_type=f32)
    answer = (line_base + jnp.dot(carried.astype(bf16), coupling_in[0], preferred_element_type=f32)).astype(bf16)
    iterate = dual_part + lax.dot_general(
        answer, basis, (((1,), (1,)), ((), ())), preferred_element_type=f32
    )
    iterate = iterate.reshape(sample_count, face_count, block_size).transpose(1, 0, 2)
    weighted = (scale[by_slot][:, None, None] * iterate).astype(bf16)
    weighted_d = [weighted[slot[d]] for d in range(4)]
    theirs = trade(weighted_d)
    summed = jnp.stack([
        (weighted_d[d].astype(f32) + jnp.dot(theirs[d], tables[d], preferred_element_type=f32)).astype(bf16)
        for d in range(4)
    ])
    return summed[by_slot][None, None]


def solution(mesh):
    placed = (
        P("sub", "coarse", None, None, None),
        P("sub", "coarse", None),
        P("sub", "coarse", None, None),
        P("sub", "coarse", None),
        P("sub", "coarse", None),
        P("sub", "coarse", None, None),
        P("sub", "coarse", None, None),
        P("sub", None, "coarse"),
        P("sub", None, None),
        P("sub", None, None),
        P("sub", None, "coarse"),
    )
    return jax.shard_map(
        per_device,
        mesh=mesh,
        in_specs=placed,
        out_specs=P("sub", "coarse", None, None, None),
        check_vma=False,
    )
```

time: 215 us -> 136 us (0.63)
  waiting for transfers between devices: 86 us -> 37.9 us
  local copies, waits for them, and re-layouts: 37 us -> 9.79 us
  matrix products: 49.5 us -> 24.4 us
  starting transfers between devices: 19 us -> 28.9 us
  between operations: 15.2 us -> 21.5 us
  other arithmetic: 0.34 us -> 6.04 us
    dot_general x30 -> x18, matrix products: 49.5 us -> 22.5 us  [the longest x1 6.07 us: per_device(): jnp.dot(flat * dual_mask, front_inverse[0, 0], preferred_element_type=f32)]
    psum x1 -> x0, waiting for transfers between devices: 21.6 us -> none  [per_device(): lax.psum(jnp.dot(coarse_residual, own_rows, preferred_element_type=jnp.fl...]
    ppermute x8 -> x12, waiting for transfers between devices: 30.5 us -> 11.1 us  [shifted(): return lax.ppermute(array, axis, pairs)]
    dynamic_slice x32 -> x1, local copies, waits for them, and re-layouts: 16.2 us -> 0.86 us  [per_device(): own_canon_order = jnp.stack([order[slot[d]] for d in range(4)])]
    another operation x1 -> x0, local copies, waits for them, and re-layouts: 14.7 us -> none  [per_device(): front_inverse[0, 0].reshape(face_count, block_size, face_count, block_size)]
    ppermute x8 -> x12, starting transfers between devices: 18.9 us -> 28.8 us  [shifted(): return lax.ppermute(array, axis, pairs)]
    all_gather x2, waiting for transfers between devices: 33.4 us -> 26.1 us  [the longest x1 26.1 us: per_device(): inflows = lax.all_gather(inflow.astype(bf16), 'sub')]
    gather x0 -> x3, local copies, waits for them, and re-layouts: none -> 3.34 us  [the longest x1 1.58 us: per_device(): return summed[by_slot][None, None]]
  transfers between devices with their start and end apart: 11 -> 14, of which waited for: 6 -> 5; matrix products, arithmetic and copies ran while one was open for 11% -> 23% of each run, Pallas kernels for 0% -> 0%
where the time goes in v1:
time: 136 us
  waiting for transfers between devices  37.9 us (28%)
  starting transfers between devices  28.9 us (21%)
  matrix products  24.4 us (18%)
  between operations  21.5 us (16%)
  local copies, waits for them, and re-layouts  9.79 us (7%)
  blocking collectives  7.19 us (5%)
  other arithmetic  6.04 us (4%)
    ppermute x12, starting transfers between devices, shifted(): return lax.ppermute(array, axis, pairs)  28.8 us
    all_gather x1, waiting for transfers between devices, per_device(): inflows = lax.all_gather(inflow.astype(bf16), 'sub')  26.1 us
    ppermute x12, waiting for transfers between devices, shifted(): return lax.ppermute(array, axis, pairs)  11.1 us
    all_gather x1, blocking collectives, per_device(): lax.all_gather(coarse_residual, 'coarse', axis=1, tiled=True)  7.19 us
    dot_general x1, matrix products, per_device(): jnp.dot(flat * dual_mask, front_inverse[0, 0], preferred_element_type=f32)  6.07 us
    dot_general x8, matrix products, per_device(): jnp.dot(theirs[d], tables[d], preferred_element_type=f32)  5.39 us
    dot_general x3, matrix products, per_device(): chain = jnp.einsum('pab,pbc->pac', chain, later, precision=HIGHEST)  3.56 us
    dot_general x1, matrix products, per_device(): lax.dot_general(answer, basis, (((1,), (1,)), ((), ())), preferred_elemen...  2.73 us
  transfers between devices with their start and end apart: 14, of which 5 were waited for; matrix products, arithmetic and copies ran while one was open for 23% of the time, Pallas kernels for 0%

profile of v1, /device:TPU:0, one launch (start us, length us, event | category | flops | bytes accessed | tf_op | source)
XLA Modules:
  0.0 135.7 jit_solution(10935054080551601829)
XLA Ops:
  6.6 0.7 all-gather.4.cloned.1.call-update
  7.3 1.5 %fusion.71 = (s32[1,1,1]{2,1,0:T(1,128)}, s32[1,1,1]{2,1,0:T(1,128)}, s32[1,1,1]{2,1,0:T(1,128)}, s32[1,1,1]{2,1,0:T(1,128)}) fusion(s32[1,1,4]{2,1,0:T(1,128)} %param.12), kind=kLoop, calls=%fused_computation.123 | loop fusion | bytes 32 | tf_op jit(solution)/shard_map/slice | solution.py:51
  16.3 0.9 constant_dynamic-slice_fusion.2
  17.2 4.9 %collective-permute-start.3 = (s32[512]{0:T(512)S(1)}, s32[512]{0:T(512)S(1)}, u32[]{:S(2)}, u32[]{:S(2)}) collective-permute-start(s32[512]{0:T(512)S(1)} %bitcast.140), channel_id=1, source_target_pairs={{0,1},{2,3},{4,5},{6,7},{8,9},{10,11},{12,13},{14,15},{16,17},{18,... | collective-permute-start | bytes 6152 | tf_op jit(solution)/shard_map/ppermute | solution.py:18
  22.0 1.3 collective-permute-start.4
  23.3 1.5 %collective-permute-start.1 = (s32[512]{0:T(512)S(1)}, s32[512]{0:T(512)S(1)}, u32[]{:S(2)}, u32[]{:S(2)}) collective-permute-start(s32[512]{0:T(512)S(1)} %bitcast.136), channel_id=1, source_target_pairs={{0,2},{2,4},{4,6},{6,8},{8,10},{10,12},{12,14},{14,16},{16,18},{18... | collective-permute-start | bytes 6152 | tf_op jit(solution)/shard_map/ppermute | solution.py:18
  24.8 1.3 collective-permute-start.2
  26.1 1.3 dynamic-slice_bitcast_fusion.6
  27.4 4.6 %collective-permute-start = (bf16[256,512]{1,0:T(8,128)(2,1)S(1)}, bf16[256,512]{1,0:T(8,128)(2,1)S(1)}, u32[]{:S(2)}, u32[]{:S(2)}) collective-permute-start(bf16[256,512]{1,0:T(8,128)(2,1)S(1)} %get-tuple-element.15), channel_id=1, source_target_pairs={{0,2},{2,4},{4,6},{6,8},{8,10},{10,12},{12,14},{14,16},{16,18},{18... | collective-permute-start | bytes 786440 | tf_op jit(solution)/shard_map/ppermute | solution.py:18
  32.1 0.7 sort.17
  32.8 0.6 fusion.70
  33.8 0.6 iota_compare_fusion.6
  34.4 1.1 gather_fusion
  35.6 1.3 collective-permute-start.5
  36.9 4.6 %collective-permute-start.6 = (bf16[256,512]{1,0:T(8,128)(2,1)S(1)}, bf16[256,512]{1,0:T(8,128)(2,1)S(1)}, u32[]{:S(2)}, u32[]{:S(2)}) collective-permute-start(bf16[256,512]{1,0:T(8,128)(2,1)S(1)} %get-tuple-element.17), channel_id=1, source_target_pairs={{0,1},{2,3},{4,5},{6,7},{8,9},{10,11},{12,13},{14,15},{16,17},{18,... | collective-permute-start | bytes 786440 | tf_op jit(solution)/shard_map/ppermute | solution.py:18
  41.4 1.3 collective-permute-start.7
  42.8 0.8 fusion.2
  43.6 0.6 iota_compare_fusion
  44.2 1.1 fusion.27
  45.3 0.9 fusion.26
  46.2 0.4 collective-permute-done.6
  46.7 1.0 fusion.25
  47.6 3.7 %collective-permute-done.7 = bf16[256,512]{1,0:T(8,128)(2,1)S(1)} collective-permute-done((bf16[256,512]{1,0:T(8,128)(2,1)S(1)}, bf16[256,512]{1,0:T(8,128)(2,1)S(1)}, u32[]{:S(2)}, u32[]{:S(2)}) %collective-permute-start.7) | collective-permute-done | bytes 262176 | tf_op jit(solution)/shard_map/ppermute | solution.py:18
  51.4 1.0 fusion.24
  52.5 0.6 gather_fusion.1
  53.2 1.3 copy.18
  54.5 0.5 copy.19
  55.1 0.5 convolution_convert_fusion
  55.6 7.2 %all_gather.12 = bf16[256,512]{1,0:T(8,128)(2,1)S(1)} all-gather(bf16[256,256]{1,0:T(8,128)(2,1)S(1)} %convolution_convert_fusion), channel_id=1, replica_groups=mesh['sub'=16,'coarse'=2] {'coarse'}, dimensions={1}, use_global_device_ids=true | all-gather | bytes 393216 | tf_op jit(solution)/shard_map/all_gather | solution.py:79
  62.8 0.8 convolution_convert_fusion.1
  63.9 6.1 %fusion.3 = f32[256,2048]{1,0:T(8,128)S(1)} fusion(bf16[256,2048]{0,1:T(8,128)(2,1)} %bitcast.130, bf16[1,1,2048,2048]{3,2,1,0:T(8,128)(2,1)} %param.16, f32[2048]{0:T(1024)S(1)} %get-tuple-element.7), kind=kOutput, calls=%fused_computation.8 | convolution fusion | flops 2148007936 | bytes 11542528 | tf_op jit(solution)/shard_map/dot_general | solution.py:82
  70.0 1.4 %broadcast_select_fusion = f32[16,128,128]{2,1,0:T(8,128)S(1)} fusion(f32[16,128,128]{2,1,0:T(8,128)} %all-gather.4.cloned.1.call-done, f32[128,128]{1,0:T(8,128)S(1)} %fusion.56, pred[16]{0:T(512)(128)(4,1)S(1)} %copy-done.10), kind=kLoop, calls=%fused_computation.76 | loop fusion | flops 262144 | bytes 2162704 | tf_op jit(solution)/shard_map/jit(_where)/select_n | solution.py:86
  71.4 1.2 fusion.30
  72.7 1.2 fusion.34
  74.0 1.2 fusion.38
  75.3 1.9 %fusion.42 = bf16[15,128,128]{2,1,0:T(8,128)(2,1)} fusion(f32[16,128,128]{2,1,0:T(8,128)S(1)} %fusion.38, f32[8,128,128]{2,1,0:T(8,128)S(1)} %broadcast_in_dim.51, f32[8,128,128]{2,1,0:T(8,128)S(1)} %slice.111), kind=kOutput, calls=%fused_computation.64 | convolution fusion | flops 377749504 | bytes 2588672 | tf_op jit(solution)/shard_map/slice | solution.py:92
  77.2 26.1 %all-gather.6.cloned.1.call-done = bf16[4096,128]{1,0:T(8,128)(2,1)} async-done(((bf16[256,128]{1,0:T(8,128)(2,1)}), bf16[4096,128]{1,0:T(8,128)(2,1)}) %all-gather.6.cloned.1.call-update) | async-done | bytes 1048592 | tf_op jit(solution)/shard_map/all_gather | solution.py:81
  103.2 2.5 %fusion.29 = bf16[256,128]{1,0:T(8,128)(2,1)} fusion(bf16[16,256,128]{2,1,0:T(8,128)(2,1)} %bitcast.147, f32[1,128,128]{2,1,0:T(8,128)S(1)} %fusion.57, bf16[15,128,128]{2,1,0:T(8,128)(2,1)} %fusion.42, pred[16]{0:T(512)(128)(4,1)S(1)} %copy-done.10), kind=kOutput, calls=%fused_computation.49 | convolution fusion | flops 135561216 | bytes 1671184 | tf_op jit(solution)/shard_map/pna,pac->nc/dot_general | solution.py:94
  105.7 2.7 %convolution_add_fusion = f32[256,2048]{1,0:T(8,128)} fusion(f32[256,2048]{1,0:T(8,128)S(1)} %fusion.3, f32[256,256]{1,0:T(8,128)S(1)} %fusion.51, bf16[256,128]{1,0:T(8,128)(2,1)} %fusion.29, bf16[1,1,2048,256]{3,2,1,0:T(8,128)(2,1)S(1)} %copy-done, bf16[1,128,256]{2,1,0:T(8,128)(2,1)S(1)} %copy-done.6), kind=kOutput, calls=%fused_computation.9 | convolution fusion | flops 285868032 | bytes 5636096 | tf_op jit(solution)/shard_map/dot_general | solution.py:97
  108.4 2.0 %fusion.6 = bf16[256,4,512]{2,0,1:T(8,128)(2,1)S(1)} fusion(f32[32,4,8,512]{3,2,1,0:T(8,128)} %bitcast.129, f32[4]{0:T(128)S(1)} %copy-done.8), kind=kLoop, calls=%fused_computation.11 | loop fusion | flops 1048576 | bytes 3145744 | tf_op jit(solution)/shard_map/convert_element_type | solution.py:101
  110.5 2.2 %collective-permute-start.8 = (bf16[256,512]{1,0:T(8,128)(2,1)S(1)}, bf16[256,512]{1,0:T(8,128)(2,1)S(1)}, u32[]{:S(2)}, u32[]{:S(2)}) collective-permute-start(bf16[256,512]{1,0:T(8,128)(2,1)S(1)} %get-tuple-element.11), channel_id=1, source_target_pairs={{0,2},{2,4},{4,6},{6,8},{8,10},{10,12},{12,14},{14,16},{16,18},{18... | collective-permute-start | bytes 786440 | tf_op jit(solution)/shard_map/ppermute | solution.py:18
  112.7 3.4 %collective-permute-start.10 = (bf16[256,512]{1,0:T(8,128)(2,1)S(1)}, bf16[256,512]{1,0:T(8,128)(2,1)S(1)}, u32[]{:S(2)}, u32[]{:S(2)}) collective-permute-start(bf16[256,512]{1,0:T(8,128)(2,1)S(1)} %get-tuple-element.12), channel_id=1, source_target_pairs={{0,1},{2,3},{4,5},{6,7},{8,9},{10,11},{12,13},{14,15},{16,17},{18,... | collective-permute-start | bytes 786440 | tf_op jit(solution)/shard_map/ppermute | solution.py:18
  116.1 1.3 collective-permute-start.11
  117.4 1.3 collective-permute-start.9
  119.1 3.1 %collective-permute-done.10 = bf16[256,512]{1,0:T(8,128)(2,1)S(1)} collective-permute-done((bf16[256,512]{1,0:T(8,128)(2,1)S(1)}, bf16[256,512]{1,0:T(8,128)(2,1)S(1)}, u32[]{:S(2)}, u32[]{:S(2)}) %collective-permute-start.10) | collective-permute-done | bytes 262176 | tf_op jit(solution)/shard_map/ppermute | solution.py:18
  122.3 0.4 fusion.21
  122.6 3.8 %collective-permute-done.11 = bf16[256,512]{1,0:T(8,128)(2,1)S(1)} collective-permute-done((bf16[256,512]{1,0:T(8,128)(2,1)S(1)}, bf16[256,512]{1,0:T(8,128)(2,1)S(1)}, u32[]{:S(2)}, u32[]{:S(2)}) %collective-permute-start.11) | collective-permute-done | bytes 262176 | tf_op jit(solution)/shard_map/ppermute | solution.py:18
  127.3 1.6 %gather_fusion.2 = bf16[4,256,512]{2,1,0:T(8,128)(2,1)} fusion(bf16[4,256,512]{2,1,0:T(8,128)(2,1)S(1)} %pad_maximum_fusion.4, s32[1024]{0:T(1024)S(1)} %pad_clamp_fusion), kind=kCustom, calls=%fused_computation.2 | custom fusion | bytes 2097168 | tf_op jit(solution)/shard_map/gather | solution.py:108
  (62 shorter events, 2.6 us)
Async XLA Ops:
  6.5 48.5 %copy-start = (bf16[1,1,2048,256]{3,2,1,0:T(8,128)(2,1)S(1)}, bf16[1,1,2048,256]{3,2,1,0:T(8,128)(2,1)}, u32[]{:S(2)}) copy-start(bf16[1,1,2048,256]{3,2,1,0:T(8,128)(2,1)} %param.17) | copy-start | bytes 3145732
  6.5 25.5 %copy-start.7 = (s32[1,1,4]{2,1,0:T(1,128)S(1)}, s32[1,1,4]{2,1,0:T(1,128)}, u32[]{:S(2)}) copy-start(s32[1,1,4]{2,1,0:T(1,128)} %param.12) | copy-start | bytes 52
  6.5 26.3 %copy-start.1 = (f32[1,1,4]{2,1,0:T(1,128)S(1)}, f32[1,1,4]{2,1,0:T(1,128)}, u32[]{:S(2)}) copy-start(f32[1,1,4]{2,1,0:T(1,128)} %param.14) | copy-start | bytes 52
  6.5 26.9 %copy-start.9 = (s32[1,1,256]{2,1,0:T(1,128)S(1)}, s32[1,1,256]{2,1,0:T(1,128)}, u32[]{:S(2)}) copy-start(s32[1,1,256]{2,1,0:T(1,128)} %param.15) | copy-start | bytes 3076
  6.5 63.4 %all-gather.4.cloned.1.call-start = ((), (), s32[]{:S(2)}) async-start(), calls=%async_computation | async-start | bytes 1114112 | tf_op jit(solution)/shard_map/all_gather | solution.py:54
  7.3 96.0 %all-gather.6.cloned.1.call-start = ((), (), s32[]{:S(2)}) async-start(), calls=%async_computation.1 | async-start | bytes 1114112 | tf_op jit(solution)/shard_map/all_gather | solution.py:81
  17.2 18.4 %collective-permute-start.3 = (s32[512]{0:T(512)S(1)}, s32[512]{0:T(512)S(1)}, u32[]{:S(2)}, u32[]{:S(2)}) collective-permute-start(s32[512]{0:T(512)S(1)} %bitcast.140), channel_id=1, source_target_pairs={{0,1},{2,3},{4,5},{6,7},{8,9},{10,11},{12,13},{14,15},{16,17},{18,... | collective-permute-start | bytes 6152 | tf_op jit(solution)/shard_map/ppermute | solution.py:18
  22.0 14.8 %collective-permute-start.4 = (s32[512]{0:T(512)S(1)}, s32[512]{0:T(512)S(1)}, u32[]{:S(2)}, u32[]{:S(2)}) collective-permute-start(s32[512]{0:T(512)S(1)} %bitcast.138), channel_id=1, source_target_pairs={{1,0},{3,2},{5,4},{7,6},{9,8},{11,10},{13,12},{15,14},{17,16},{19,... | collective-permute-start | bytes 6152 | tf_op jit(solution)/shard_map/ppermute | solution.py:18
  23.3 18.1 %collective-permute-start.1 = (s32[512]{0:T(512)S(1)}, s32[512]{0:T(512)S(1)}, u32[]{:S(2)}, u32[]{:S(2)}) collective-permute-start(s32[512]{0:T(512)S(1)} %bitcast.136), channel_id=1, source_target_pairs={{0,2},{2,4},{4,6},{6,8},{8,10},{10,12},{12,14},{14,16},{16,18},{18... | collective-permute-start | bytes 6152 | tf_op jit(solution)/shard_map/ppermute | solution.py:18
  24.8 17.9 %collective-permute-start.2 = (s32[512]{0:T(512)S(1)}, s32[512]{0:T(512)S(1)}, u32[]{:S(2)}, u32[]{:S(2)}) collective-permute-start(s32[512]{0:T(512)S(1)} %bitcast.134), channel_id=1, source_target_pairs={{2,0},{4,2},{6,4},{8,6},{10,8},{12,10},{14,12},{16,14},{18,16},{20... | collective-permute-start | bytes 6152 | tf_op jit(solution)/shard_map/ppermute | solution.py:18
  27.4 16.8 %collective-permute-start = (bf16[256,512]{1,0:T(8,128)(2,1)S(1)}, bf16[256,512]{1,0:T(8,128)(2,1)S(1)}, u32[]{:S(2)}, u32[]{:S(2)}) collective-permute-start(bf16[256,512]{1,0:T(8,128)(2,1)S(1)} %get-tuple-element.15), channel_id=1, source_target_pairs={{0,2},{2,4},{4,6},{6,8},{8,10},{10,12},{12,14},{14,16},{16,18},{18... | collective-permute-start | bytes 786440 | tf_op jit(solution)/shard_map/ppermute | solution.py:18
  35.6 9.7 %collective-permute-start.5 = (bf16[256,512]{1,0:T(8,128)(2,1)S(1)}, bf16[256,512]{1,0:T(8,128)(2,1)S(1)}, u32[]{:S(2)}, u32[]{:S(2)}) collective-permute-start(bf16[256,512]{1,0:T(8,128)(2,1)S(1)} %get-tuple-element.16), channel_id=1, source_target_pairs={{2,0},{4,2},{6,4},{8,6},{10,8},{12,10},{14,12},{16,14},{18,16},{20... | collective-permute-start | bytes 786440 | tf_op jit(solution)/shard_map/ppermute | solution.py:18
  36.9 9.8 %collective-permute-start.6 = (bf16[256,512]{1,0:T(8,128)(2,1)S(1)}, bf16[256,512]{1,0:T(8,128)(2,1)S(1)}, u32[]{:S(2)}, u32[]{:S(2)}) collective-permute-start(bf16[256,512]{1,0:T(8,128)(2,1)S(1)} %get-tuple-element.17), channel_id=1, source_target_pairs={{0,1},{2,3},{4,5},{6,7},{8,9},{10,11},{12,13},{14,15},{16,17},{18,... | collective-permute-start | bytes 786440 | tf_op jit(solution)/shard_map/ppermute | solution.py:18
  41.4 10.0 %collective-permute-start.7 = (bf16[256,512]{1,0:T(8,128)(2,1)S(1)}, bf16[256,512]{1,0:T(8,128)(2,1)S(1)}, u32[]{:S(2)}, u32[]{:S(2)}) collective-permute-start(bf16[256,512]{1,0:T(8,128)(2,1)S(1)} %get-tuple-element.18), channel_id=1, source_target_pairs={{1,0},{3,2},{5,4},{7,6},{9,8},{11,10},{13,12},{15,14},{17,16},{19,... | collective-permute-start | bytes 786440 | tf_op jit(solution)/shard_map/ppermute | solution.py:18
  44.2 7.2 %copy-start.2 = (pred[4,512,512]{2,1,0:T(32,128)(4,1)}, pred[4,512,512]{2,1,0:T(32,128)(4,1)S(1)}, u32[]{:S(2)}) copy-start(pred[4,512,512]{2,1,0:T(32,128)(4,1)S(1)} %iota_compare_fusion) | copy-start | bytes 3145732
  54.5 9.1 %copy-start.4 = (bf16[1,512,256]{2,1,0:T(8,128)(2,1)S(1)}, bf16[1,512,256]{2,1,0:T(8,128)(2,1)}, u32[]{:S(2)}) copy-start(bf16[1,512,256]{2,1,0:T(8,128)(2,1)} %param.18) | copy-start | bytes 786436
  55.1 7.7 %copy-start.5 = (bf16[1,512,128]{2,1,0:T(8,128)(2,1)S(1)}, bf16[1,512,128]{2,1,0:T(8,128)(2,1)}, u32[]{:S(2)}) copy-start(bf16[1,512,128]{2,1,0:T(8,128)(2,1)} %param.19) | copy-start | bytes 393220
  63.9 6.1 %copy-start.10 = (pred[16]{0:T(512)(128)(4,1)S(1)}, pred[16]{0:T(512)(128)(4,1)}, u32[]{:S(2)}) copy-start(pred[16]{0:T(512)(128)(4,1)} %iota_compare_fusion.6) | copy-start | bytes 52
  77.2 28.5 %copy-start.6 = (bf16[1,128,256]{2,1,0:T(8,128)(2,1)S(1)}, bf16[1,128,256]{2,1,0:T(8,128)(2,1)}, u32[]{:S(2)}) copy-start(bf16[1,128,256]{2,1,0:T(8,128)(2,1)} %param.21) | copy-start | bytes 196612
  105.7 2.7 %copy-start.8 = (f32[4]{0:T(128)S(1)}, f32[4]{0:T(128)}, u32[]{:S(2)}) copy-start(f32[4]{0:T(128)} %gather_fusion) | copy-start | bytes 52
  108.4 10.3 %copy-start.3 = (pred[4,512,512]{2,1,0:T(32,128)(4,1)S(1)}, pred[4,512,512]{2,1,0:T(32,128)(4,1)}, u32[]{:S(2)}) copy-start(pred[4,512,512]{2,1,0:T(32,128)(4,1)} %copy-done.2) | copy-start | bytes 3145732
  110.5 8.2 %collective-permute-start.8 = (bf16[256,512]{1,0:T(8,128)(2,1)S(1)}, bf16[256,512]{1,0:T(8,128)(2,1)S(1)}, u32[]{:S(2)}, u32[]{:S(2)}) collective-permute-start(bf16[256,512]{1,0:T(8,128)(2,1)S(1)} %get-tuple-element.11), channel_id=1, source_target_pairs={{0,2},{2,4},{4,6},{6,8},{8,10},{10,12},{12,14},{14,16},{16,18},{18... | collective-permute-start | bytes 786440 | tf_op jit(solution)/shard_map/ppermute | solution.py:18
  112.7 9.5 %collective-permute-start.10 = (bf16[256,512]{1,0:T(8,128)(2,1)S(1)}, bf16[256,512]{1,0:T(8,128)(2,1)S(1)}, u32[]{:S(2)}, u32[]{:S(2)}) collective-permute-start(bf16[256,512]{1,0:T(8,128)(2,1)S(1)} %get-tuple-element.12), channel_id=1, source_target_pairs={{0,1},{2,3},{4,5},{6,7},{8,9},{10,11},{12,13},{14,15},{16,17},{18,... | collective-permute-start | bytes 786440 | tf_op jit(solution)/shard_map/ppermute | solution.py:18
  116.1 10.3 %collective-permute-start.11 = (bf16[256,512]{1,0:T(8,128)(2,1)S(1)}, bf16[256,512]{1,0:T(8,128)(2,1)S(1)}, u32[]{:S(2)}, u32[]{:S(2)}) collective-permute-start(bf16[256,512]{1,0:T(8,128)(2,1)S(1)} %get-tuple-element.13), channel_id=1, source_target_pairs={{1,0},{3,2},{5,4},{7,6},{9,8},{11,10},{13,12},{15,14},{17,16},{19,... | collective-permute-start | bytes 786440 | tf_op jit(solution)/shard_map/ppermute | solution.py:18
  117.4 9.3 %collective-permute-start.9 = (bf16[256,512]{1,0:T(8,128)(2,1)S(1)}, bf16[256,512]{1,0:T(8,128)(2,1)S(1)}, u32[]{:S(2)}, u32[]{:S(2)}) collective-permute-start(bf16[256,512]{1,0:T(8,128)(2,1)S(1)} %get-tuple-element.14), channel_id=1, source_target_pairs={{2,0},{4,2},{6,4},{8,6},{10,8},{12,10},{14,12},{16,14},{18,16},{20... | collective-permute-start | bytes 786440 | tf_op jit(solution)/shard_map/ppermute | solution.py:18
Sparse Core Ops, SparseCore 0:
  9.5 42.4 all-gather.3
  64.0 39.2 all-gather.5

commit v2 on v1

v2 whole, which is shorter than its diff:
```python
import functools

import jax
import jax.numpy as jnp
from jax import lax
from jax.experimental import pallas as pl
from jax.experimental.pallas import tpu as pltpu
from jax.sharding import PartitionSpec as P

MESH = pl.DeviceIdType.MESH
F32, BF16 = jnp.float32, jnp.bfloat16
NT = (((1,), (1,)), ((), ()))


def dot(a, b):
    return jnp.dot(a, b, preferred_element_type=F32)


def dot_nt(a, b):
    return lax.dot_general(a, b, NT, preferred_element_type=F32)


def split_rows(x):
    high = x.astype(BF16).astype(F32)
    return jnp.concatenate([high, x - high], axis=0).astype(BF16)


def kernel(
    peers,
    lines,
    slot_ref,
    scale_ref,
    parts_ref,
    order_ref,
    primal_ref,
    transfer_ref,
    inverse_hbm,
    basis_hbm,
    line_hbm,
    handoff_hbm,
    coupling_hbm,
    out_ref,
    inverse,
    basis,
    line,
    handoff,
    coupling,
    face_out,
    face_in,
    order_out,
    order_in,
    table,
    placed,
    residual,
    dual,
    mask,
    coarse,
    transfers,
    inflow,
    heat_in,
    heat_out,
    carried,
    weighted,
    face_out2,
    face_in2,
    load_sem,
    face_send,
    face_recv,
    order_send,
    order_recv,
    coarse_send,
    coarse_recv,
    chip_send,
    chip_recv,
    core_send,
    core_recv,
    heat_send,
    heat_recv,
    back_send,
    back_recv,
    face_send2,
    face_recv2,
):
    me, col = lax.axis_index("sub"), lax.axis_index("coarse")
    faces, samples, block = parts_ref.shape
    primal = basis.shape[1]
    rows = samples // peers
    chips = peers // 2
    chip, core = me // 2, lax.rem(me, 2)

    loads = [
        pltpu.make_async_copy(source, target, load_sem.at[i])
        for i, (source, target) in enumerate(
            [
                (basis_hbm, basis),
                (inverse_hbm, inverse),
                (handoff_hbm, handoff),
                (line_hbm, line),
                (coupling_hbm, coupling),
            ]
        )
    ]
    for load in loads:
        load.start()

    barrier = pltpu.get_barrier_semaphore()

    @pl.loop(1, peers)
    def _(k):
        pl.semaphore_signal(
            barrier, inc=1, device_id=(lax.rem(me + k, peers), col), device_id_type=MESH
        )

    @pl.loop(1, lines)
    def _(k):
        pl.semaphore_signal(
            barrier, inc=1, device_id=(me, lax.rem(col + k, lines)), device_id_type=MESH
        )

    slots = [slot_ref[d] for d in range(4)]
    direction = []
    for s in range(4):
        found = jnp.int32(0)
        for d in range(1, 4):
            found = jnp.where(slots[d] == s, d, found)
        direction.append(found)
    scales = [scale_ref[direction[s]] for s in range(4)]

    for d in range(4):
        face_out[d] = parts_ref[slots[d]]
        own = order_ref[pl.ds(slots[d], 1), :]
        order_out[d] = jnp.broadcast_to(own, (8, block))
    transfers[core, chip] = transfer_ref[...].astype(BF16)

    pl.semaphore_wait(barrier, peers - 1 + lines - 1)

    exists = [me > 0, me < peers - 1, col > 0, col < lines - 1]
    beside = [
        (jnp.maximum(me - 1, 0), col),
        (jnp.minimum(me + 1, peers - 1), col),
        (me, jnp.maximum(col - 1, 0)),
        (me, jnp.minimum(col + 1, lines - 1)),
    ]

    def face_copy(source, target, send, recv, d, at):
        return pltpu.make_async_remote_copy(
            src_ref=source.at[d],
            dst_ref=target.at[at],
            send_sem=send.at[d],
            recv_sem=recv.at[at],
            device_id=beside[d],
            device_id_type=MESH,
        )

    def orders(d, at):
        return face_copy(order_out, order_in, order_send, order_recv, d, at)

    def first(d, at):
        return face_copy(face_out, face_in, face_send, face_recv, d, at)

    def second(d, at):
        return face_copy(face_out2, face_in2, face_send2, face_recv2, d, at)

    for d in (2, 3, 0, 1):

        @pl.when(exists[d])
        def _():
            orders(d, d ^ 1).start()
            first(d, d ^ 1).start()

    def to_chip(target, source):
        return pltpu.make_async_remote_copy(
            src_ref=transfers.at[core, source],
            dst_ref=transfers.at[core, source],
            send_sem=chip_send.at[target],
            recv_sem=chip_recv.at[source],
            device_id=(target * 2 + core, col),
            device_id_type=MESH,
        )

    @pl.loop(1, chips)
    def _(k):
        to_chip(lax.rem(chip + k, chips), chip).start()

    ids = primal_ref[...]
    count = ids.shape[1]
    groups = faces * block // 128
    group_hit = jnp.where(lax.broadcasted_iota(jnp.int32, (groups, count), 0) == ids // 128, 1.0, 0.0)
    lane_hit = jnp.where(lax.broadcasted_iota(jnp.int32, (128, count), 0) == ids % 128, 1.0, 0.0)
    kept = 1.0 - dot_nt(group_hit.astype(BF16), lane_hit.astype(BF16))
    per_face = block // 128
    for s in range(4):
        row = jnp.concatenate(
            [kept[s * per_face + t : s * per_face + t + 1] for t in range(per_face)], axis=1
        )
        mask[s] = jnp.broadcast_to(row, (8, block))

    for d in (0, 1, 2, 3):

        @pl.when(exists[d])
        def _():
            position = lax.broadcasted_iota(jnp.int32, (block, block), 0)
            own_table = jnp.where(position == order_out[d, 0:1, :], 1.0, 0.0).astype(BF16)
            orders(d, d).wait_recv()
            theirs = order_in[d]
            halves = jnp.concatenate([theirs // 16, theirs % 16], axis=0)
            found = dot_nt(halves.astype(F32).astype(BF16), own_table)
            joined = (found[0:1] * 16.0 + found[8:9]).astype(jnp.int32)
            table[d] = jnp.where(position == joined, 1.0, 0.0).astype(BF16)

    def place(d, copy, landed):
        @pl.when(exists[d])
        def _():
            copy(d, d).wait_recv()
            placed[d] = dot(landed[d], table[d]).astype(BF16)

        @pl.when(jnp.logical_not(exists[d]))
        def _():
            placed[d] = jnp.zeros((samples, block), BF16)

    for d in (0, 1, 2, 3):
        place(d, first, face_in)
    for s in range(4):
        total = parts_ref[s].astype(F32) + placed[direction[s]].astype(F32)
        residual[:, s * block : (s + 1) * block] = (scales[s] * total).astype(BF16)

    loads[0].wait()
    own_coarse = dot(residual[...], basis[...])
    coarse[col] = own_coarse.astype(BF16)

    def to_line(target, source):
        return pltpu.make_async_remote_copy(
            src_ref=coarse.at[source],
            dst_ref=coarse.at[source],
            send_sem=coarse_send.at[target],
            recv_sem=coarse_recv.at[source],
            device_id=(me, target),
            device_id_type=MESH,
        )

    @pl.loop(1, lines)
    def _(k):
        to_line(lax.rem(col + k, lines), col).start()

    @pl.loop(1, chips)
    def _(k):
        to_chip(chip, lax.rem(chip + k, chips)).wait_recv()

    def to_core(which):
        return pltpu.make_async_remote_copy(
            src_ref=transfers.at[which],
            dst_ref=transfers.at[which],
            send_sem=core_send,
            recv_sem=core_recv,
            device_id=(chip * 2 + 1 - core, col),
            device_id_type=MESH,
        )

    to_core(core).start()

    for s in range(4):
        at = slice(s * block, (s + 1) * block)
        residual[:, at] = (residual[:, at].astype(F32) * mask[s, 0:1, :]).astype(BF16)
    loads[1].wait()

    @pl.loop(0, 4)
    def _(s):
        at = pl.ds(pl.multiple_of(s * block, block), block)
        dual[s] = dot(residual[...], inverse[:, at]) * mask[s, 0:1, :]

    loads[2].wait()

    @pl.loop(1, lines)
    def _(k):
        to_line(col, lax.rem(col + k, lines)).wait_recv()

    heat = jnp.zeros((samples, handoff.shape[1]), F32)
    for q in range(lines):
        heat += dot(coarse[q], handoff[q * primal : (q + 1) * primal, :])
    inflow[...] = heat

    def to_samples(target, source):
        return pltpu.make_async_remote_copy(
            src_ref=inflow.at[pl.ds(pl.multiple_of(target * rows, rows), rows)],
            dst_ref=heat_in.at[source],
            send_sem=heat_send.at[target],
            recv_sem=heat_recv.at[source],
            device_id=(target, col),
            device_id_type=MESH,
        )

    @pl.loop(1, peers)
    def _(k):
        to_samples(lax.rem(me + k, peers), me).start()

    heat_in[me] = inflow[pl.ds(pl.multiple_of(me * rows, rows), rows), :]

    loads[3].wait()
    base = jnp.zeros((samples, primal), F32)
    for q in range(lines):
        base += dot(coarse[q], line[q * primal : (q + 1) * primal, :])

    to_core(1 - core).wait_recv()

    def to_lines(target, source):
        return pltpu.make_async_remote_copy(
            src_ref=heat_out.at[target],
            dst_ref=carried.at[pl.ds(pl.multiple_of(source * rows, rows), rows)],
            send_sem=back_send.at[target],
            recv_sem=back_recv.at[source],
            device_id=(target, col),
            device_id_type=MESH,
        )

    def advance(p, state):
        heat_out[p] = state

        @pl.when(p != me)
        def _():
            to_lines(p, me).start()
            to_samples(me, p).wait_recv()

        split = dot(split_rows(state), transfers[lax.rem(p, 2), p // 2])
        return split[:rows] + split[rows:] + heat_in[p]

    lax.fori_loop(0, peers, advance, jnp.zeros((rows, handoff.shape[1]), F32))
    carried[pl.ds(pl.multiple_of(me * rows, rows), rows), :] = heat_out[me]
    loads[4].wait()

    @pl.loop(1, peers)
    def _(k):
        to_lines(me, lax.rem(me + k, peers)).wait_recv()

    coupled = dot(split_rows(carried[...]), coupling[...])
    answer = (base + coupled[:samples] + coupled[samples:]).astype(BF16)
    for s in range(4):
        found = dual[s] + dot_nt(answer, basis[s * block : (s + 1) * block, :])
        weighted[s] = (scales[s] * found).astype(BF16)
    for d in (2, 3, 0, 1):
        face_out2[d] = weighted[slots[d]]

        @pl.when(exists[d])
        def _():
            second(d, d ^ 1).start()

    for d in (0, 1, 2, 3):
        place(d, second, face_in2)
    for s in range(4):
        total = weighted[s].astype(F32) + placed[direction[s]].astype(F32)
        out_ref[s] = total.astype(BF16)

    for d in range(4):

        @pl.when(exists[d])
        def _():
            orders(d, d ^ 1).wait_send()
            first(d, d ^ 1).wait_send()
            second(d, d ^ 1).wait_send()

    @pl.loop(1, chips)
    def _(k):
        to_chip(lax.rem(chip + k, chips), chip).wait_send()

    to_core(core).wait_send()

    @pl.loop(1, lines)
    def _(k):
        to_line(lax.rem(col + k, lines), col).wait_send()

    @pl.loop(1, peers)
    def _(k):
        to_samples(lax.rem(me + k, peers), me).wait_send()
        to_lines(lax.rem(me + k, peers), me).wait_send()


def per_device(
    peers,
    lines,
    residual_parts,
    face_slot,
    face_order,
    face_scale,
    vertex_unknowns,
    front_inverse,
    coarse_basis,
    coarse_inverse,
    thermal_handoff,
    chain_transfer,
    coupling_in,
):
    faces, samples, block = residual_parts.shape[2:]
    interface = faces * block
    primal = coarse_basis.shape[-1]
    channels = chain_transfer.shape[-1]
    rows = samples // peers
    dma = pltpu.SemaphoreType.DMA
    vmem, smem, hbm = (
        pl.BlockSpec(memory_space=space) for space in (pltpu.VMEM, pltpu.SMEM, pl.ANY)
    )
    stack = pltpu.VMEM((faces, samples, block), BF16)
    out = pl.pallas_call(
        functools.partial(kernel, peers, lines),
        out_shape=jax.ShapeDtypeStruct((faces, samples, block), BF16),
        in_specs=[smem] * 2 + [vmem] * 4 + [hbm] * 5,
        out_specs=vmem,
        scratch_shapes=[
            pltpu.VMEM((interface, interface), BF16),
            pltpu.VMEM((interface, primal), BF16),
            pltpu.VMEM((lines * primal, primal), BF16),
            pltpu.VMEM((lines * primal, channels), BF16),
            pltpu.VMEM((channels, primal), BF16),
            stack,
            stack,
            pltpu.VMEM((faces, 8, block), jnp.int32),
            pltpu.VMEM((faces, 8, block), jnp.int32),
            pltpu.VMEM((faces, block, block), BF16),
            stack,
            pltpu.VMEM((samples, interface), BF16),
            pltpu.VMEM((faces, samples, block), F32),
            pltpu.VMEM((faces, 8, block), F32),
            pltpu.VMEM((lines, samples, primal), BF16),
            pltpu.VMEM((2, peers // 2, channels, channels), BF16),
            pltpu.VMEM((samples, channels), F32),
            pltpu.VMEM((peers, rows, channels), F32),
            pltpu.VMEM((peers, rows, channels), F32),
            pltpu.VMEM((samples, channels), F32),
            stack,
            stack,
            stack,
            dma((5,)),
            dma((4,)),
            dma((4,)),
            dma((4,)),
            dma((4,)),
            dma((lines,)),
            dma((lines,)),
            dma((peers // 2,)),
            dma((peers // 2,)),
            dma,
            dma,
            dma((peers,)),
            dma((peers,)),
            dma((peers,)),
            dma((peers,)),
            dma((4,)),
            dma((4,)),
        ],
        compiler_params=pltpu.CompilerParams(
            collective_id=0, has_side_effects=True, vmem_limit_bytes=48 * 1024 * 1024
        ),
    )(
        face_slot[0, 0],
        face_scale[0, 0],
        residual_parts[0, 0],
        face_order[0, 0],
        vertex_unknowns[0],
        chain_transfer[0],
        front_inverse[0, 0],
        coarse_basis[0, 0],
        coarse_inverse[0],
        thermal_handoff[0],
        coupling_in[0],
    )
    return out[None, None]


def solution(mesh):
    placed = (
        P("sub", "coarse", None, None, None),
        P("sub", "coarse", None),
        P("sub", "coarse", None, None),
        P("sub", "coarse", None),
        P("sub", "coarse", None),
        P("sub", "coarse", None, None),
        P("sub", "coarse", None, None),
        P("sub", None, "coarse"),
        P("sub", None, None),
        P("sub", None, None),
        P("sub", None, "coarse"),
    )
    return jax.shard_map(
        functools.partial(per_device, mesh.shape["sub"], mesh.shape["coarse"]),
        mesh=mesh,
        in_specs=placed,
        out_specs=P("sub", "coarse", None, None, None),
        check_vma=False,
    )
```

time: 136 us -> 51.3 us (0.38)
  the two profiles are of different devices: /device:TPU:0 before, /device:TPU:9 now
where the time goes in v2:
time: 51.3 us; the launch traced here: 50.9 us
  Pallas kernels  41.3 us (81%)
  local copies, waits for them, and re-layouts  9.64 us (19%)
    pallas_call x1, Pallas kernels, per_device(): pl.pallas_call(functools.partial(kernel, peers, lines), out_shape=jax.Sha...  41.3 us
    unnamed x21, local copies, waits for them, and re-layouts  9.64 us

profile of v2, /device:TPU:9, one launch (start us, length us, event | category | flops | bytes accessed | tf_op | source)
XLA Modules:
  0.0 50.9 jit_solution(9886974466259326156)
XLA Ops:
  0.0 0.0 copy-start
  0.0 1.2 %copy-done = bf16[1,1,4,256,512]{4,3,2,1,0:T(8,128)(2,1)S(1)} copy-done((bf16[1,1,4,256,512]{4,3,2,1,0:T(8,128)(2,1)S(1)}, bf16[1,1,4,256,512]{4,3,2,1,0:T(8,128)(2,1)}, u32[]{:S(2)}) %copy-start) | copy-done | bytes 1048600
  1.2 0.0 copy-start.1
  1.2 1.2 %copy-done.1 = bf16[1,1,2048,256]{3,2,1,0:T(8,128)(2,1)S(1)} copy-done((bf16[1,1,2048,256]{3,2,1,0:T(8,128)(2,1)S(1)}, bf16[1,1,2048,256]{3,2,1,0:T(8,128)(2,1)}, u32[]{:S(2)}) %copy-start.1) | copy-done | bytes 1048600
  2.5 0.0 copy-start.2
  2.5 0.9 %copy-done.2 = bf16[1,512,256]{2,1,0:T(8,128)(2,1)S(1)} copy-done((bf16[1,512,256]{2,1,0:T(8,128)(2,1)S(1)}, bf16[1,512,256]{2,1,0:T(8,128)(2,1)}, u32[]{:S(2)}) %copy-start.2) | copy-done | bytes 262168
  3.4 0.0 copy-start.3
  3.4 0.9 %copy-done.3 = bf16[1,512,128]{2,1,0:T(8,128)(2,1)S(1)} copy-done((bf16[1,512,128]{2,1,0:T(8,128)(2,1)S(1)}, bf16[1,512,128]{2,1,0:T(8,128)(2,1)}, u32[]{:S(2)}) %copy-start.3) | copy-done | bytes 131096
  4.3 0.0 copy-start.4
  4.3 0.8 %copy-done.4 = f32[1,128,128]{2,1,0:T(8,128)S(1)} copy-done((f32[1,128,128]{2,1,0:T(8,128)S(1)}, f32[1,128,128]{2,1,0:T(8,128)}, u32[]{:S(2)}) %copy-start.4) | copy-done | bytes 65560
  5.1 0.0 copy-start.5
  5.1 0.8 %copy-done.5 = bf16[1,128,256]{2,1,0:T(8,128)(2,1)S(1)} copy-done((bf16[1,128,256]{2,1,0:T(8,128)(2,1)S(1)}, bf16[1,128,256]{2,1,0:T(8,128)(2,1)}, u32[]{:S(2)}) %copy-start.5) | copy-done | bytes 65560
  6.0 0.0 copy-start.6
  6.0 0.7 %copy-done.6 = s32[1,1,4,512]{3,2,1,0:T(4,128)S(1)} copy-done((s32[1,1,4,512]{3,2,1,0:T(4,128)S(1)}, s32[1,1,4,512]{3,2,1,0:T(4,128)}, u32[]{:S(2)}) %copy-start.6) | copy-done | bytes 8216
  6.7 0.0 copy-start.7
  6.7 0.7 %copy-done.7 = s32[1,1,256]{2,1,0:T(1,128)S(1)} copy-done((s32[1,1,256]{2,1,0:T(1,128)S(1)}, s32[1,1,256]{2,1,0:T(1,128)}, u32[]{:S(2)}) %copy-start.7) | copy-done | bytes 1048
  7.4 0.0 copy-start.8
  7.4 0.7 %copy-done.8 = s32[1,1,4]{2,1,0:T(1,128)S(1)} copy-done((s32[1,1,4]{2,1,0:T(1,128)S(1)}, s32[1,1,4]{2,1,0:T(1,128)}, u32[]{:S(2)}) %copy-start.8) | copy-done | bytes 40
  8.0 0.0 copy-start.9
  8.0 0.7 %copy-done.9 = f32[1,1,4]{2,1,0:T(1,128)S(1)} copy-done((f32[1,1,4]{2,1,0:T(1,128)S(1)}, f32[1,1,4]{2,1,0:T(1,128)}, u32[]{:S(2)}) %copy-start.9) | copy-done | bytes 40
  8.7 41.3 %shard_map.109 = bf16[4,256,512]{2,1,0:T(8,128)(2,1)S(1)} custom-call(s32[4]{0:T(128)S(1)} %bitcast.21, f32[4]{0:T(128)S(1)} %bitcast.22, bf16[4,256,512]{2,1,0:T(8,128)(2,1)S(1)} %bitcast.13, s32[4,512]{1,0:T(4,128)S(1)} %bitcast.19, s32[1,256]{1,0:T(1,128)S(1)} %bitcast.20, f32[128,128]{1,0:T(8,128)S(1)} %bitcast.17, bf16[2048,2048]{1,0:T(8,128)(2,1)} %bitcast.23, ...), custom_call_target="tpu_custom_call" | custom-call | tf_op jit(solution)/shard_map/pallas_call | solution.py:401
  50.0 1.0 %copy.13 = bf16[1,1,4,256,512]{4,3,2,1,0:T(8,128)(2,1)} copy(bf16[1,1,4,256,512]{4,3,2,1,0:T(8,128)(2,1)S(1)} %bitcast.12) | data formatting | bytes 2097152
Async XLA Ops:
  0.0 1.2 %copy-start = (bf16[1,1,4,256,512]{4,3,2,1,0:T(8,128)(2,1)S(1)}, bf16[1,1,4,256,512]{4,3,2,1,0:T(8,128)(2,1)}, u32[]{:S(2)}) copy-start(bf16[1,1,4,256,512]{4,3,2,1,0:T(8,128)(2,1)} %param.11) | copy-start | bytes 3145732
  1.2 1.2 %copy-start.1 = (bf16[1,1,2048,256]{3,2,1,0:T(8,128)(2,1)S(1)}, bf16[1,1,2048,256]{3,2,1,0:T(8,128)(2,1)}, u32[]{:S(2)}) copy-start(bf16[1,1,2048,256]{3,2,1,0:T(8,128)(2,1)} %param.17) | copy-start | bytes 3145732
  2.5 0.9 %copy-start.2 = (bf16[1,512,256]{2,1,0:T(8,128)(2,1)S(1)}, bf16[1,512,256]{2,1,0:T(8,128)(2,1)}, u32[]{:S(2)}) copy-start(bf16[1,512,256]{2,1,0:T(8,128)(2,1)} %param.18) | copy-start | bytes 786436
  3.4 0.9 %copy-start.3 = (bf16[1,512,128]{2,1,0:T(8,128)(2,1)S(1)}, bf16[1,512,128]{2,1,0:T(8,128)(2,1)}, u32[]{:S(2)}) copy-start(bf16[1,512,128]{2,1,0:T(8,128)(2,1)} %param.19) | copy-start | bytes 393220
  4.3 0.8 %copy-start.4 = (f32[1,128,128]{2,1,0:T(8,128)S(1)}, f32[1,128,128]{2,1,0:T(8,128)}, u32[]{:S(2)}) copy-start(f32[1,128,128]{2,1,0:T(8,128)} %param.20) | copy-start | bytes 196612
  5.1 0.8 %copy-start.5 = (bf16[1,128,256]{2,1,0:T(8,128)(2,1)S(1)}, bf16[1,128,256]{2,1,0:T(8,128)(2,1)}, u32[]{:S(2)}) copy-start(bf16[1,128,256]{2,1,0:T(8,128)(2,1)} %param.21) | copy-start | bytes 196612
  6.0 0.7 %copy-start.6 = (s32[1,1,4,512]{3,2,1,0:T(4,128)S(1)}, s32[1,1,4,512]{3,2,1,0:T(4,128)}, u32[]{:S(2)}) copy-start(s32[1,1,4,512]{3,2,1,0:T(4,128)} %param.13) | copy-start | bytes 24580
  6.7 0.7 %copy-start.7 = (s32[1,1,256]{2,1,0:T(1,128)S(1)}, s32[1,1,256]{2,1,0:T(1,128)}, u32[]{:S(2)}) copy-start(s32[1,1,256]{2,1,0:T(1,128)} %param.15) | copy-start | bytes 3076
  7.4 0.7 %copy-start.8 = (s32[1,1,4]{2,1,0:T(1,128)S(1)}, s32[1,1,4]{2,1,0:T(1,128)}, u32[]{:S(2)}) copy-start(s32[1,1,4]{2,1,0:T(1,128)} %param.12) | copy-start | bytes 52
  8.0 0.7 %copy-start.9 = (f32[1,1,4]{2,1,0:T(1,128)S(1)}, f32[1,1,4]{2,1,0:T(1,128)}, u32[]{:S(2)}) copy-start(f32[1,1,4]{2,1,0:T(1,128)} %param.14) | copy-start | bytes 52

commit v3 on v2

--- a/solution.py
+++ b/solution.py
@@ -25,21 +25,32 @@
     return jnp.concatenate([high, x - high], axis=0).astype(BF16)
 
 
+def shares(samples, peers, lines):
+    rows = samples // peers
+    return lines if rows % (8 * lines) == 0 else 1
+
+
 def kernel(
     peers,
     lines,
+    slot_hbm,
+    scale_hbm,
+    parts_hbm,
+    order_hbm,
+    primal_hbm,
+    transfer_hbm,
+    inverse_hbm,
+    basis_hbm,
+    line_hbm,
+    handoff_hbm,
+    coupling_hbm,
+    out_ref,
     slot_ref,
     scale_ref,
     parts_ref,
     order_ref,
     primal_ref,
     transfer_ref,
-    inverse_hbm,
-    basis_hbm,
-    line_hbm,
-    handoff_hbm,
-    coupling_hbm,
-    out_ref,
     inverse,
     basis,
     line,
@@ -56,6 +67,8 @@
     mask,
     coarse,
     transfers,
+    within,
+    through,
     inflow,
     heat_in,
     heat_out,
@@ -84,7 +97,8 @@
     me, col = lax.axis_index("sub"), lax.axis_index("coarse")
     faces, samples, block = parts_ref.shape
     primal = basis.shape[1]
-    rows = samples // peers
+    share = shares(samples, peers, lines)
+    rows = samples // (peers * share)
     chips = peers // 2
     chip, core = me // 2, lax.rem(me, 2)
 
@@ -92,9 +106,15 @@
         pltpu.make_async_copy(source, target, load_sem.at[i])
         for i, (source, target) in enumerate(
             [
+                (slot_hbm, slot_ref),
+                (scale_hbm, scale_ref),
+                (parts_hbm, parts_ref),
+                (order_hbm, order_ref),
+                (transfer_hbm, transfer_ref),
+                (primal_hbm, primal_ref),
                 (basis_hbm, basis),
+                (handoff_hbm, handoff),
                 (inverse_hbm, inverse),
-                (handoff_hbm, handoff),
                 (line_hbm, line),
                 (coupling_hbm, coupling),
             ]
@@ -105,18 +125,23 @@
 
     barrier = pltpu.get_barrier_semaphore()
 
-    @pl.loop(1, peers)
-    def _(k):
-        pl.semaphore_signal(
-            barrier, inc=1, device_id=(lax.rem(me + k, peers), col), device_id_type=MESH
-        )
-
-    @pl.loop(1, lines)
-    def _(k):
-        pl.semaphore_signal(
-            barrier, inc=1, device_id=(me, lax.rem(col + k, lines)), device_id_type=MESH
-        )
-
+    def other(n):
+        return lax.rem(me + lax.rem(n, peers), peers), lax.rem(col + n // peers, lines)
+
+    @pl.loop(1, peers * share)
+    def _(n):
+        pl.semaphore_signal(barrier, inc=1, device_id=other(n), device_id_type=MESH)
+
+    if share == 1:
+
+        @pl.loop(1, lines)
+        def _(k):
+            pl.semaphore_signal(
+                barrier, inc=1, device_id=(me, lax.rem(col + k, lines)), device_id_type=MESH
+            )
+
+    for load in loads[:5]:
+        load.wait()
     slots = [slot_ref[d] for d in range(4)]
     direction = []
     for s in range(4):
@@ -132,7 +157,7 @@
         order_out[d] = jnp.broadcast_to(own, (8, block))
     transfers[core, chip] = transfer_ref[...].astype(BF16)
 
-    pl.semaphore_wait(barrier, peers - 1 + lines - 1)
+    pl.semaphore_wait(barrier, peers * share - 1 + (lines - 1 if share == 1 else 0))
 
     exists = [me > 0, me < peers - 1, col > 0, col < lines - 1]
     beside = [
@@ -182,6 +207,7 @@
     def _(k):
         to_chip(lax.rem(chip + k, chips), chip).start()
 
+    loads[5].wait()
     ids = primal_ref[...]
     count = ids.shape[1]
     groups = faces * block // 128
@@ -224,7 +250,7 @@
         total = parts_ref[s].astype(F32) + placed[direction[s]].astype(F32)
         residual[:, s * block : (s + 1) * block] = (scales[s] * total).astype(BF16)
 
-    loads[0].wait()
+    loads[6].wait()
     own_coarse = dot(residual[...], basis[...])
     coarse[col] = own_coarse.astype(BF16)
 
@@ -238,9 +264,63 @@
             device_id_type=MESH,
         )
 
-    @pl.loop(1, lines)
-    def _(k):
-        to_line(lax.rem(col + k, lines), col).start()
+    def line_start():
+        @pl.loop(1, lines)
+        def _(k):
+            to_line(lax.rem(col + k, lines), col).start()
+
+    def line_wait():
+        @pl.loop(1, lines)
+        def _(k):
+            to_line(col, lax.rem(col + k, lines)).wait_recv()
+
+    def place_of(p, c):
+        return (c if share > 1 else 0) * peers + p
+
+    def chunk(p, c):
+        first_row = (p * share + (c if share > 1 else 0)) * rows
+        return pl.ds(pl.multiple_of(first_row, rows), rows)
+
+    def to_samples(target, source):
+        return pltpu.make_async_remote_copy(
+            src_ref=inflow.at[chunk(*target)],
+            dst_ref=heat_in.at[place_of(*source)],
+            send_sem=heat_send.at[place_of(*target)],
+            recv_sem=heat_recv.at[place_of(*source)],
+            device_id=target,
+            device_id_type=MESH,
+        )
+
+    def to_lines(target, source):
+        return pltpu.make_async_remote_copy(
+            src_ref=heat_out.at[target[0]],
+            dst_ref=carried.at[chunk(*source)],
+            send_sem=back_send.at[place_of(*target)],
+            recv_sem=back_recv.at[place_of(*source)],
+            device_id=target,
+            device_id_type=MESH,
+        )
+
+    here = (me, col)
+    loads[7].wait()
+    if share > 1:
+        own_rows = pl.ds(pl.multiple_of(col * primal, primal), primal)
+        inflow[...] = dot(coarse[col], handoff[own_rows, :])
+    else:
+        line_start()
+        line_wait()
+        heat = jnp.zeros((samples, handoff.shape[1]), F32)
+        for q in range(lines):
+            heat += dot(coarse[q], handoff[q * primal : (q + 1) * primal, :])
+        inflow[...] = heat
+
+    @pl.loop(1, peers * share)
+    def _(n):
+        to_samples(other(n), here).start()
+
+    if share > 1:
+        line_start()
+    heat_in[place_of(*here)] = inflow[chunk(*here), :]
 
     @pl.loop(1, chips)
     def _(k):
@@ -261,75 +341,84 @@
     for s in range(4):
         at = slice(s * block, (s + 1) * block)
         residual[:, at] = (residual[:, at].astype(F32) * mask[s, 0:1, :]).astype(BF16)
-    loads[1].wait()
-
-    @pl.loop(0, 4)
-    def _(s):
+    loads[8].wait()
+
+    def dual_face(s):
         at = pl.ds(pl.multiple_of(s * block, block), block)
         dual[s] = dot(residual[...], inverse[:, at]) * mask[s, 0:1, :]
 
-    loads[2].wait()
-
-    @pl.loop(1, lines)
-    def _(k):
-        to_line(col, lax.rem(col + k, lines)).wait_recv()
-
-    heat = jnp.zeros((samples, handoff.shape[1]), F32)
-    for q in range(lines):
-        heat += dot(coarse[q], handoff[q * primal : (q + 1) * primal, :])
-    inflow[...] = heat
-
-    def to_samples(target, source):
-        return pltpu.make_async_remote_copy(
-            src_ref=inflow.at[pl.ds(pl.multiple_of(target * rows, rows), rows)],
-            dst_ref=heat_in.at[source],
-            send_sem=heat_send.at[target],
-            recv_sem=heat_recv.at[source],
-            device_id=(target, col),
-            device_id_type=MESH,
-        )
-
-    @pl.loop(1, peers)
-    def _(k):
-        to_samples(lax.rem(me + k, peers), me).start()
-
-    heat_in[me] = inflow[pl.ds(pl.multiple_of(me * rows, rows), rows), :]
-
-    loads[3].wait()
+    pl.loop(0, 2)(dual_face)
+
+    to_core(1 - core).wait_recv()
+    width = handoff.shape[1]
+    groups4 = peers // 4
+    nothing = jnp.zeros((width, width), BF16)
+    for g in range(groups4):
+        t0, t1 = transfers[0, 2 * g], transfers[1, 2 * g]
+        t2, t3 = transfers[0, 2 * g + 1], transfers[1, 2 * g + 1]
+        t01 = dot(t0, t1).astype(BF16)
+        t12 = dot(t1, t2).astype(BF16)
+        t23 = dot(t2, t3).astype(BF16)
+        t012 = dot(t01, t2).astype(BF16)
+        t123 = dot(t12, t3).astype(BF16)
+        t0123 = dot(t012, t3).astype(BF16)
+        for k, tile in enumerate((t0, t01, t012, t0123)):
+            through[g, :, k * width : (k + 1) * width] = tile
+        table3 = ((t1, t12, t123), (nothing, t2, t23), (nothing, nothing, t3))
+        for i in range(3):
+            for k in range(3):
+                within[g, i * width : (i + 1) * width, k * width : (k + 1) * width] = table3[i][k]
+
+    @pl.loop(1, peers * share)
+    def _(n):
+        to_samples(here, other(n)).wait_recv()
+
+    local = []
+    for g in range(groups4):
+        own = []
+        for i in range(4):
+            total = heat_in[4 * g + i]
+            for c in range(1, share):
+                total = total + heat_in[c * peers + 4 * g + i]
+            own.append(total)
+        split = dot(split_rows(jnp.concatenate(own[:3], axis=1)), within[g])
+        split = split[:rows] + split[rows:]
+        local.append(
+            [own[0]] + [split[:, k * width : (k + 1) * width] + own[k + 1] for k in range(3)]
+        )
+    state = jnp.zeros((rows, width), F32)
+    for g in range(groups4):
+        heat_out[4 * g] = state
+        split = dot(split_rows(state), through[g])
+        split = split[:rows] + split[rows:]
+        ahead = [split[:, k * width : (k + 1) * width] + local[g][k] for k in range(4)]
+        for k in range(3):
+            heat_out[4 * g + k + 1] = ahead[k]
+        state = ahead[3]
+
+        @pl.loop(0, 4 * share)
+        def _(n):
+            p, c = 4 * g + lax.rem(n, 4), n // 4
+
+            @pl.when(jnp.logical_or(p != me, c != 0))
+            def _():
+                to_lines((p, lax.rem(col + c, lines)), here).start()
+
+    carried[chunk(*here), :] = heat_out[me]
+
+    pl.loop(2, 4)(dual_face)
+
+    if share > 1:
+        line_wait()
+    loads[9].wait()
     base = jnp.zeros((samples, primal), F32)
     for q in range(lines):
         base += dot(coarse[q], line[q * primal : (q + 1) * primal, :])
-
-    to_core(1 - core).wait_recv()
-
-    def to_lines(target, source):
-        return pltpu.make_async_remote_copy(
-            src_ref=heat_out.at[target],
-            dst_ref=carried.at[pl.ds(pl.multiple_of(source * rows, rows), rows)],
-            send_sem=back_send.at[target],
-            recv_sem=back_recv.at[source],
-            device_id=(target, col),
-            device_id_type=MESH,
-        )
-
-    def advance(p, state):
-        heat_out[p] = state
-
-        @pl.when(p != me)
-        def _():
-            to_lines(p, me).start()
-            to_samples(me, p).wait_recv()
-
-        split = dot(split_rows(state), transfers[lax.rem(p, 2), p // 2])
-        return split[:rows] + split[rows:] + heat_in[p]
-
-    lax.fori_loop(0, peers, advance, jnp.zeros((rows, handoff.shape[1]), F32))
-    carried[pl.ds(pl.multiple_of(me * rows, rows), rows), :] = heat_out[me]
-    loads[4].wait()
-
-    @pl.loop(1, peers)
-    def _(k):
-        to_lines(me, lax.rem(me + k, peers)).wait_recv()
+    loads[10].wait()
+
+    @pl.loop(1, peers * share)
+    def _(n):
+        to_lines(here, other(n)).wait_recv()
 
     coupled = dot(split_rows(carried[...]), coupling[...])
     answer = (base + coupled[:samples] + coupled[samples:]).astype(BF16)
@@ -367,10 +456,10 @@
     def _(k):
         to_line(lax.rem(col + k, lines), col).wait_send()
 
-    @pl.loop(1, peers)
-    def _(k):
-        to_samples(lax.rem(me + k, peers), me).wait_send()
-        to_lines(lax.rem(me + k, peers), me).wait_send()
+    @pl.loop(1, peers * share)
+    def _(n):
+        to_samples(other(n), here).wait_send()
+        to_lines(other(n), here).wait_send()
 
 
 def per_device(
@@ -392,18 +481,23 @@
     interface = faces * block
     primal = coarse_basis.shape[-1]
     channels = chain_transfer.shape[-1]
-    rows = samples // peers
+    share = shares(samples, peers, lines)
+    rows = samples // (peers * share)
     dma = pltpu.SemaphoreType.DMA
-    vmem, smem, hbm = (
-        pl.BlockSpec(memory_space=space) for space in (pltpu.VMEM, pltpu.SMEM, pl.ANY)
-    )
+    vmem, hbm = (pl.BlockSpec(memory_space=space) for space in (pltpu.VMEM, pltpu.HBM))
     stack = pltpu.VMEM((faces, samples, block), BF16)
     out = pl.pallas_call(
         functools.partial(kernel, peers, lines),
         out_shape=jax.ShapeDtypeStruct((faces, samples, block), BF16),
-        in_specs=[smem] * 2 + [vmem] * 4 + [hbm] * 5,
+        in_specs=[hbm] * 11,
         out_specs=vmem,
         scratch_shapes=[
+            pltpu.SMEM((faces,), jnp.int32),
+            pltpu.SMEM((faces,), F32),
+            stack,
+            pltpu.VMEM((faces, block), jnp.int32),
+            pltpu.VMEM((1, vertex_unknowns.shape[-1]), jnp.int32),
+            pltpu.VMEM((channels, channels), F32),
             pltpu.VMEM((interface, interface), BF16),
             pltpu.VMEM((interface, primal), BF16),
             pltpu.VMEM((lines * primal, primal), BF16),
@@ -420,14 +514,16 @@
             pltpu.VMEM((faces, 8, block), F32),
             pltpu.VMEM((lines, samples, primal), BF16),
             pltpu.VMEM((2, peers // 2, channels, channels), BF16),
+            pltpu.VMEM((peers // 4, 3 * channels, 3 * channels), BF16),
+            pltpu.VMEM((peers // 4, channels, 4 * channels), BF16),
             pltpu.VMEM((samples, channels), F32),
-            pltpu.VMEM((peers, rows, channels), F32),
+            pltpu.VMEM((share * peers, rows, channels), F32),
             pltpu.VMEM((peers, rows, channels), F32),
             pltpu.VMEM((samples, channels), F32),
             stack,
             stack,
             stack,
-            dma((5,)),
+            dma((11,)),
             dma((4,)),
             dma((4,)),
             dma((4,)),
@@ -438,15 +534,15 @@
             dma((peers // 2,)),
             dma,
             dma,
-            dma((peers,)),
-            dma((peers,)),
-            dma((peers,)),
-            dma((peers,)),
+            dma((share * peers,)),
+            dma((share * peers,)),
+            dma((share * peers,)),
+            dma((share * peers,)),
             dma((4,)),
             dma((4,)),
         ],
         compiler_params=pltpu.CompilerParams(
-            collective_id=0, has_side_effects=True, vmem_limit_bytes=48 * 1024 * 1024
+            collective_id=0, has_side_effects=True, vmem_limit_bytes=60 * 1024 * 1024
         ),
     )(
         face_slot[0, 0],

time: 51.3 us -> 43.9 us (0.86)
  the two profiles are of different devices: /device:TPU:9 before, /device:TPU:0 now
where the time goes in v3:
time: 43.9 us; the launch traced here: 43.7 us
  Pallas kernels  41.5 us (95%)
  local copies, waits for them, and re-layouts  2.26 us (5%)
    pallas_call x1, Pallas kernels, per_device(): pl.pallas_call(functools.partial(kernel, peers, lines), out_shape=jax.Sha...  41.5 us
    unnamed x1, local copies, waits for them, and re-layouts  2.26 us

profile of v3, /device:TPU:0, one launch (start us, length us, event | category | flops | bytes accessed | tf_op | source)
XLA Modules:
  0.0 43.7 jit_solution(3889957114536546986)
XLA Ops:
  0.0 41.5 %shard_map.109 = bf16[4,256,512]{2,1,0:T(8,128)(2,1)} custom-call(s32[4]{0:T(128)} %bitcast.22, f32[4]{0:T(128)} %bitcast.23, bf16[4,256,512]{2,1,0:T(8,128)(2,1)} %bitcast.14, s32[4,512]{1,0:T(4,128)} %bitcast.20, s32[1,256]{1,0:T(1,128)} %bitcast.21, f32[128,128]{1,0:T(8,128)} %bitcast.18, bf16[2048,2048]{1,0:T(8,128)(2,1)} %bitcast.12, ...), custom_call_target="tpu_custom_call" | custom-call | tf_op jit(solution)/shard_map/pallas_call | solution.py:489
  41.5 2.3 %copy.13 = bf16[1,1,4,256,512]{4,3,2,1,0:T(8,128)(2,1)} copy(bf16[1,1,4,256,512]{4,3,2,1,0:T(8,128)(2,1)} %bitcast.13) | data formatting | bytes 2097152

commit v4 on v3

--- a/solution.py
+++ b/solution.py
@@ -197,8 +197,8 @@
         return pltpu.make_async_remote_copy(
             src_ref=transfers.at[core, source],
             dst_ref=transfers.at[core, source],
-            send_sem=chip_send.at[target],
-            recv_sem=chip_recv.at[source],
+            send_sem=chip_send,
+            recv_sem=chip_recv,
             device_id=(target * 2 + core, col),
             device_id_type=MESH,
         )
@@ -285,8 +285,8 @@
         return pltpu.make_async_remote_copy(
             src_ref=inflow.at[chunk(*target)],
             dst_ref=heat_in.at[place_of(*source)],
-            send_sem=heat_send.at[place_of(*target)],
-            recv_sem=heat_recv.at[place_of(*source)],
+            send_sem=heat_send,
+            recv_sem=heat_recv,
             device_id=target,
             device_id_type=MESH,
         )
@@ -295,11 +295,23 @@
         return pltpu.make_async_remote_copy(
             src_ref=heat_out.at[target[0]],
             dst_ref=carried.at[chunk(*source)],
-            send_sem=back_send.at[place_of(*target)],
-            recv_sem=back_recv.at[place_of(*source)],
+            send_sem=back_send,
+            recv_sem=back_recv,
             device_id=target,
             device_id_type=MESH,
         )
+
+    def await_bytes(part, sem):
+        pltpu.make_async_copy(part, part, sem).wait()
+
+    def await_chips(sem):
+        await_bytes(transfers.at[0, pl.ds(0, chips - 1)], sem)
+
+    def await_heat(sem):
+        await_bytes(heat_in.at[pl.ds(0, peers * share - 1)], sem)
+
+    def await_back(sem):
+        await_bytes(carried.at[pl.ds(0, (peers * share - 1) * rows)], sem)
 
     here = (me, col)
     loads[7].wait()
@@ -322,9 +334,7 @@
         line_start()
     heat_in[place_of(*here)] = inflow[chunk(*here), :]
 
-    @pl.loop(1, chips)
-    def _(k):
-        to_chip(chip, lax.rem(chip + k, chips)).wait_recv()
+    await_chips(chip_recv)
 
     def to_core(which):
         return pltpu.make_async_remote_copy(
@@ -369,9 +379,7 @@
             for k in range(3):
                 within[g, i * width : (i + 1) * width, k * width : (k + 1) * width] = table3[i][k]
 
-    @pl.loop(1, peers * share)
-    def _(n):
-        to_samples(here, other(n)).wait_recv()
+    await_heat(heat_recv)
 
     local = []
     for g in range(groups4):
@@ -416,9 +424,7 @@
         base += dot(coarse[q], line[q * primal : (q + 1) * primal, :])
     loads[10].wait()
 
-    @pl.loop(1, peers * share)
-    def _(n):
-        to_lines(here, other(n)).wait_recv()
+    await_back(back_recv)
 
     coupled = dot(split_rows(carried[...]), coupling[...])
     answer = (base + coupled[:samples] + coupled[samples:]).astype(BF16)
@@ -446,9 +452,7 @@
             first(d, d ^ 1).wait_send()
             second(d, d ^ 1).wait_send()
 
-    @pl.loop(1, chips)
-    def _(k):
-        to_chip(lax.rem(chip + k, chips), chip).wait_send()
+    await_chips(chip_send)
 
     to_core(core).wait_send()
 
@@ -456,10 +460,8 @@
     def _(k):
         to_line(lax.rem(col + k, lines), col).wait_send()
 
-    @pl.loop(1, peers * share)
-    def _(n):
-        to_samples(other(n), here).wait_send()
-        to_lines(other(n), here).wait_send()
+    await_heat(heat_send)
+    await_back(back_send)
 
 
 def per_device(
@@ -488,7 +490,7 @@
     stack = pltpu.VMEM((faces, samples, block), BF16)
     out = pl.pallas_call(
         functools.partial(kernel, peers, lines),
-        out_shape=jax.ShapeDtypeStruct((faces, samples, block), BF16),
+        out_shape=pltpu.VMEM((faces, samples, block), BF16),
         in_specs=[hbm] * 11,
         out_specs=vmem,
         scratch_shapes=[
@@ -530,14 +532,14 @@
             dma((4,)),
             dma((lines,)),
             dma((lines,)),
-            dma((peers // 2,)),
-            dma((peers // 2,)),
-            dma,
-            dma,
-            dma((share * peers,)),
-            dma((share * peers,)),
-            dma((share * peers,)),
-            dma((share * peers,)),
+            dma,
+            dma,
+            dma,
+            dma,
+            dma,
+            dma,
+            dma,
+            dma,
             dma((4,)),
             dma((4,)),
         ],

time: 43.9 us -> 39.7 us (0.904)
  Pallas kernels: 41.5 us -> 38.5 us
  local copies, waits for them, and re-layouts: 2.26 us -> 0.97 us
    pallas_call x1, Pallas kernels: 41.5 us -> 38.5 us  [per_device(): pl.pallas_call(functools.partial(kernel, peers, lines), out_shape=pltpu.V...]
    unnamed x1, local copies, waits for them, and re-layouts: 2.26 us -> 0.97 us
where the time goes in v4:
time: 39.7 us; the launch traced here: 39.5 us
  Pallas kernels  38.5 us (97%)
  local copies, waits for them, and re-layouts  0.97 us (2%)
    pallas_call x1, Pallas kernels, per_device(): pl.pallas_call(functools.partial(kernel, peers, lines), out_shape=pltpu.V...  38.5 us
    unnamed x1, local copies, waits for them, and re-layouts  0.97 us

profile of v4, /device:TPU:0, one launch (start us, length us, event | category | flops | bytes accessed | tf_op | source)
XLA Modules:
  0.0 39.5 jit_solution(1931504069421549410)
XLA Ops:
  0.0 38.5 %shard_map.109 = bf16[4,256,512]{2,1,0:T(8,128)(2,1)S(1)} custom-call(s32[4]{0:T(128)} %bitcast.22, f32[4]{0:T(128)} %bitcast.23, bf16[4,256,512]{2,1,0:T(8,128)(2,1)} %bitcast.14, s32[4,512]{1,0:T(4,128)} %bitcast.20, s32[1,256]{1,0:T(1,128)} %bitcast.21, f32[128,128]{1,0:T(8,128)} %bitcast.18, bf16[2048,2048]{1,0:T(8,128)(2,1)} %bitcast.13, ...), custom_call_target="tpu_custom_call" | custom-call | tf_op jit(solution)/shard_map/pallas_call | solution.py:491
  38.6 1.0 %copy.13 = bf16[1,1,4,256,512]{4,3,2,1,0:T(8,128)(2,1)} copy(bf16[1,1,4,256,512]{4,3,2,1,0:T(8,128)(2,1)S(1)} %bitcast.12) | data formatting | bytes 2097152

commit v5 on v4

--- a/solution.py
+++ b/solution.py
@@ -76,6 +76,10 @@
     weighted,
     face_out2,
     face_in2,
+    basis_out,
+    basis_in,
+    answer_out,
+    answer_in,
     load_sem,
     face_send,
     face_recv,
@@ -93,10 +97,14 @@
     back_recv,
     face_send2,
     face_recv2,
+    basis_send,
+    basis_recv,
+    answer_send,
+    answer_recv,
 ):
     me, col = lax.axis_index("sub"), lax.axis_index("coarse")
     faces, samples, block = parts_ref.shape
-    primal = basis.shape[1]
+    primal = basis.shape[2]
     share = shares(samples, peers, lines)
     rows = samples // (peers * share)
     chips = peers // 2
@@ -186,6 +194,19 @@
     def second(d, at):
         return face_copy(face_out2, face_in2, face_send2, face_recv2, d, at)
 
+    def bases(d, at):
+        return face_copy(basis_out, basis_in, basis_send, basis_recv, d, at)
+
+    def answers(d, at):
+        return pltpu.make_async_remote_copy(
+            src_ref=answer_out,
+            dst_ref=answer_in.at[at],
+            send_sem=answer_send.at[d],
+            recv_sem=answer_recv.at[at],
+            device_id=beside[d],
+            device_id_type=MESH,
+        )
+
     for d in (2, 3, 0, 1):
 
         @pl.when(exists[d])
@@ -251,7 +272,7 @@
         residual[:, s * block : (s + 1) * block] = (scales[s] * total).astype(BF16)
 
     loads[6].wait()
-    own_coarse = dot(residual[...], basis[...])
+    own_coarse = dot(residual[...], basis[...].reshape(faces * block, primal))
     coarse[col] = own_coarse.astype(BF16)
 
     def to_line(target, source):
@@ -332,6 +353,13 @@
 
     if share > 1:
         line_start()
+    for d in range(4):
+        basis_out[d] = basis[slots[d]]
+
+        @pl.when(exists[d])
+        def _():
+            bases(d, d ^ 1).start()
+
     heat_in[place_of(*here)] = inflow[chunk(*here), :]
 
     await_chips(chip_recv)
@@ -357,7 +385,13 @@
         at = pl.ds(pl.multiple_of(s * block, block), block)
         dual[s] = dot(residual[...], inverse[:, at]) * mask[s, 0:1, :]
 
-    pl.loop(0, 2)(dual_face)
+    pl.loop(0, 4)(dual_face)
+    for d in (2, 3, 0, 1):
+        face_out2[d] = dual[slots[d]].astype(BF16)
+
+        @pl.when(exists[d])
+        def _():
+            second(d, d ^ 1).start()
 
     to_core(1 - core).wait_recv()
     width = handoff.shape[1]
@@ -414,8 +448,6 @@
 
     carried[chunk(*here), :] = heat_out[me]
 
-    pl.loop(2, 4)(dual_face)
-
     if share > 1:
         line_wait()
     loads[9].wait()
@@ -428,18 +460,28 @@
 
     coupled = dot(split_rows(carried[...]), coupling[...])
     answer = (base + coupled[:samples] + coupled[samples:]).astype(BF16)
+    answer_out[...] = answer
+    for d in (2, 3, 0, 1):
+
+        @pl.when(exists[d])
+        def _():
+            answers(d, d ^ 1).start()
+
     for s in range(4):
-        found = dual[s] + dot_nt(answer, basis[s * block : (s + 1) * block, :])
+        found = dual[s] + dot_nt(answer, basis[s])
         weighted[s] = (scales[s] * found).astype(BF16)
-    for d in (2, 3, 0, 1):
-        face_out2[d] = weighted[slots[d]]
-
-        @pl.when(exists[d])
-        def _():
-            second(d, d ^ 1).start()
 
     for d in (0, 1, 2, 3):
-        place(d, second, face_in2)
+
+        @pl.when(exists[d])
+        def _():
+            bases(d, d).wait_recv()
+            second(d, d).wait_recv()
+            answers(d, d).wait_recv()
+            theirs = face_in2[d].astype(F32) + dot_nt(answer_in[d], basis_in[d])
+            theirs = ((1.0 - scale_ref[d]) * theirs).astype(BF16)
+            placed[d] = dot(theirs, table[d]).astype(BF16)
+
     for s in range(4):
         total = weighted[s].astype(F32) + placed[direction[s]].astype(F32)
         out_ref[s] = total.astype(BF16)
@@ -451,6 +493,8 @@
             orders(d, d ^ 1).wait_send()
             first(d, d ^ 1).wait_send()
             second(d, d ^ 1).wait_send()
+            bases(d, d ^ 1).wait_send()
+            answers(d, d ^ 1).wait_send()
 
     await_chips(chip_send)
 
@@ -501,7 +545,7 @@
             pltpu.VMEM((1, vertex_unknowns.shape[-1]), jnp.int32),
             pltpu.VMEM((channels, channels), F32),
             pltpu.VMEM((interface, interface), BF16),
-            pltpu.VMEM((interface, primal), BF16),
+            pltpu.VMEM((faces, block, primal), BF16),
             pltpu.VMEM((lines * primal, primal), BF16),
             pltpu.VMEM((lines * primal, channels), BF16),
             pltpu.VMEM((channels, primal), BF16),
@@ -525,6 +569,10 @@
             stack,
             stack,
             stack,
+            pltpu.VMEM((faces, block, primal), BF16),
+            pltpu.VMEM((faces, block, primal), BF16),
+            pltpu.VMEM((samples, primal), BF16),
+            pltpu.VMEM((faces, samples, primal), BF16),
             dma((11,)),
             dma((4,)),
             dma((4,)),
@@ -540,6 +588,10 @@
             dma,
             dma,
             dma,
+            dma((4,)),
+            dma((4,)),
+            dma((4,)),
+            dma((4,)),
             dma((4,)),
             dma((4,)),
         ],
@@ -554,7 +606,7 @@
         vertex_unknowns[0],
         chain_transfer[0],
         front_inverse[0, 0],
-        coarse_basis[0, 0],
+        coarse_basis[0, 0].reshape(faces, block, primal),
         coarse_inverse[0],
         thermal_handoff[0],
         coupling_in[0],

time: 39.7 us -> 42.8 us (1.078)
  Pallas kernels: 38.5 us -> 41.6 us
    pallas_call x1, Pallas kernels: 38.5 us -> 41.6 us  [per_device(): pl.pallas_call(functools.partial(kernel, peers, lines), out_shape=pltpu.V...]
where the time goes in v5:
time: 42.8 us; the launch traced here: 42.6 us
  Pallas kernels  41.6 us (97%)
  local copies, waits for them, and re-layouts  0.97 us (2%)
    pallas_call x1, Pallas kernels, per_device(): pl.pallas_call(functools.partial(kernel, peers, lines), out_shape=pltpu.V...  41.6 us
    unnamed x1, local copies, waits for them, and re-layouts  0.97 us

profile of v5, /device:TPU:0, one launch (start us, length us, event | category | flops | bytes accessed | tf_op | source)
XLA Modules:
  0.0 42.6 jit_solution(7944951879167066717)
XLA Ops:
  0.0 41.6 %shard_map.109 = bf16[4,256,512]{2,1,0:T(8,128)(2,1)S(1)} custom-call(s32[4]{0:T(128)} %bitcast.22, f32[4]{0:T(128)} %bitcast.23, bf16[4,256,512]{2,1,0:T(8,128)(2,1)} %bitcast.14, s32[4,512]{1,0:T(4,128)} %bitcast.20, s32[1,256]{1,0:T(1,128)} %bitcast.21, f32[128,128]{1,0:T(8,128)} %bitcast.18, bf16[2048,2048]{1,0:T(8,128)(2,1)} %bitcast.13, ...), custom_call_target="tpu_custom_call" | custom-call | tf_op jit(solution)/shard_map/pallas_call | solution.py:535
  41.6 1.0 %copy.13 = bf16[1,1,4,256,512]{4,3,2,1,0:T(8,128)(2,1)} copy(bf16[1,1,4,256,512]{4,3,2,1,0:T(8,128)(2,1)S(1)} %bitcast.12) | data formatting | bytes 2097152
